TPU v7x, 32 devices: a whole 2x2x4 slice. The times are simulated.
32 devices in a mesh: expert: 4 (over y, x), cuts: 8 (over z, core).
Axes of the slice: x: 2, y: 2, z: 4, core: 2. Of those that a mesh axis runs over, the one named last changes fastest.
Arguments:
- tokens: bfloat16 [4, 2, 1024, 1024], P('expert', None, 'cuts'), may hold values from -6 to 6
- cotangent: bfloat16 [4, 2, 1024, 1024], P('expert', None, 'cuts'), may hold values from -6 to 6
- segments: int32 [4, 2, 1024], P('expert'), may hold values from 0 to 2, as said below
- expert_ids: int32 [4, 2, 1024], P('expert', None, 'cuts'), may hold values from 0 to 3
- slot_ids: int32 [4, 2, 1024], P('expert', None, 'cuts'), may hold values from 0 to 40, as said below
- kept_mask: int32 [4, 2, 1024], P('expert', None, 'cuts'), may hold values from 0 to 1, as said below
- norm1_gain: bfloat16 [1024], replicated, may hold values from 0.25 to 1.75
- w_query: bfloat16 [1024, 1024], replicated, may hold values from -0.1875 to 0.1875
- w_key: bfloat16 [1024, 1024], replicated, may hold values from -0.1875 to 0.1875
- w_value: bfloat16 [1024, 1024], replicated, may hold values from -0.1875 to 0.1875
- w_output: bfloat16 [1024, 1024], replicated, may hold values from -1.5 to 1.5
- norm2_gain: bfloat16 [1024], replicated, may hold values from 0.25 to 1.75
- dense_in: bfloat16 [1024, 4096], replicated, may hold values from -0.1875 to 0.1875
- dense_out: bfloat16 [4096, 1024], replicated, may hold values from -0.09375 to 0.09375
- router: bfloat16 [1024, 4], replicated, may hold values from -0.125 to 0.125
- mixer: bfloat16 [1024, 2], replicated, may hold values from -0.1875 to 0.1875
- expert_in: bfloat16 [4, 1024, 4096], P('expert', None, 'cuts'), may hold values from -0.1875 to 0.1875
- expert_out: bfloat16 [4, 4096, 1024], P('expert', 'cuts'), may hold values from -3 to 3
Outputs:
- output: bfloat16 [4, 2, 1024, 1024], P('expert', None, 'cuts')
- grad_tokens: float32 [4, 2, 1024, 1024], P('expert', None, 'cuts')
- grad_norm1: float32 [1024], P(('expert', 'cuts'))
- grad_query: float32 [1024, 1024], P(('expert', 'cuts'))
- grad_key: float32 [1024, 1024], P(('expert', 'cuts'))
- grad_value: float32 [1024, 1024], P(('expert', 'cuts'))
- grad_output: float32 [1024, 1024], P(('expert', 'cuts'))
- grad_norm2: float32 [1024], P(('expert', 'cuts'))
- grad_dense_in: float32 [1024, 4096], P(('expert', 'cuts'))
- grad_dense_out: float32 [4096, 1024], P(('expert', 'cuts'))
- grad_router: float32 [1024, 4], P(('expert', 'cuts'))
- grad_mixer: float32 [1024, 2], P(('expert', 'cuts'))
- grad_expert_in: float32 [4, 1024, 4096], P('expert', None, 'cuts')
- grad_expert_out: float32 [4, 4096, 1024], P('expert', 'cuts')
Inputs may be any that keep to these rules, and one draw needn't show every extreme that they name: `segments`: document numbers never fall along a sequence; in every sequence the document numbered 1 begins within the first 128 positions and ends within the last 128. `slot_ids`: the rank of a token among the tokens of its block of 128 positions that go to the same expert, in order of position, or 40 where that rank is 40 or more. In every micro-batch one expert has more than 40 tokens in every block. `kept_mask`: 1 exactly where slot_ids is under 40.
All inputs are finite; a program needn't handle non-finite values.
Results may differ from a plain program's by a relative error of at most 0.02.
Values may be sent and summed in bfloat16 or wider, within the bound.
A program may use at most 256 MiB of HBM per device.

v0:
```python
from functools import partial

import jax
import jax.numpy as jnp
from jax import lax
from jax.sharding import PartitionSpec as P

score_scale = 0.125
masked_value = -1e30
norm_eps = 1e-05


def layer_norm(values, gain):
    center = values - jnp.mean(values, axis=-1, keepdims=True)
    spread = jnp.mean(center * center, axis=-1, keepdims=True)
    return center * lax.rsqrt(spread + norm_eps) * gain


def gelu_exact(values):
    return jax.nn.gelu(values, approximate=False)


def gelu_grad(values, upstream):
    return jax.vjp(gelu_exact, values)[1](upstream)[0]


def softmax_rows(values):
    raised = jnp.exp(values - jnp.max(values, axis=-1, keepdims=True))
    return raised / jnp.sum(raised, axis=-1, keepdims=True)


def plain_dot(left, right):
    return jnp.dot(left, right, preferred_element_type=jnp.float32)


def lead_dot(left, right):
    return lax.dot_general(
        left, right, (((0,), (0,)), ((), ())), preferred_element_type=jnp.float32
    )


def tail_dot(left, right):
    return lax.dot_general(
        left, right, (((1,), (1,)), ((), ())), preferred_element_type=jnp.float32
    )


def split_heads(values):
    return values.reshape(values.shape[0], values.shape[1] // 64, 64)


def mix_rows(norm_rows, router_w, mixer_w, dense_rows, expert_part, residual, hot_mask, kept_rows):
    logits = jnp.dot(
        norm_rows, router_w, precision=lax.Precision.HIGHEST, preferred_element_type=jnp.float32
    )
    gate_value = jnp.sum(jnp.where(hot_mask, softmax_rows(logits), 0.0), axis=-1) * kept_rows
    mixing = softmax_rows(
        jnp.dot(
            norm_rows, mixer_w, precision=lax.Precision.HIGHEST, preferred_element_type=jnp.float32
        )
    )
    return (
        residual
        + mixing[..., 0:1] * dense_rows
        + mixing[..., 1:2] * gate_value[..., None] * expert_part
    )


def key_block(keys_all, values_all, docs_all, block_index, row_count):
    start = block_index * row_count
    return (
        split_heads(lax.dynamic_slice_in_dim(keys_all, start, row_count, 0)),
        split_heads(lax.dynamic_slice_in_dim(values_all, start, row_count, 0)),
        start + jnp.arange(row_count, dtype=jnp.int32),
        lax.dynamic_slice_in_dim(docs_all, start, row_count, 0),
    )


def masked_scores(query_heads, key_heads, query_spots, key_spots, query_docs, key_docs):
    raw = (
        jnp.einsum("qhd,khd->hqk", query_heads, key_heads, preferred_element_type=jnp.float32)
        * score_scale
    )
    allowed = (key_spots[None, :] <= query_spots[:, None]) & (
        key_docs[None, :] == query_docs[:, None]
    )
    return jnp.where(allowed[None], raw, masked_value)


def probs_pair(
    query_heads,
    back_heads,
    logsum,
    key_heads,
    value_heads,
    query_spots,
    key_spots,
    query_docs,
    key_docs,
):
    probs = jnp.exp(
        masked_scores(query_heads, key_heads, query_spots, key_spots, query_docs, key_docs)
        - logsum[..., None]
    )
    dprobs = jnp.einsum("qhd,khd->hqk", back_heads, value_heads, preferred_element_type=jnp.float32)
    return (probs, dprobs)


def score_grads(probs, dprobs, delta):
    return (probs * (dprobs - delta[..., None])).astype(jnp.bfloat16)


def attend_forward(query, keys_all, values_all, docs_all, cut_index, row_count):
    query_heads = split_heads(query)
    head_count = query_heads.shape[1]
    query_spots = cut_index * row_count + jnp.arange(row_count, dtype=jnp.int32)
    query_docs = lax.dynamic_slice_in_dim(docs_all, cut_index * row_count, row_count, 0)

    def stats_step(block_index, carry):
        top, total = carry
        key_heads, value_heads, key_spots, key_docs = key_block(
            keys_all, values_all, docs_all, block_index, row_count
        )
        masked = masked_scores(query_heads, key_heads, query_spots, key_spots, query_docs, key_docs)
        new_top = jnp.maximum(top, jnp.max(masked, axis=-1))
        total = total * jnp.exp(top - new_top) + jnp.sum(
            jnp.exp(masked - new_top[..., None]), axis=-1
        )
        return (new_top, total)

    start_top = jnp.full((head_count, row_count), masked_value, jnp.float32)
    top, total = lax.fori_loop(
        0, cut_index + 1, stats_step, (start_top, jnp.zeros((head_count, row_count), jnp.float32))
    )
    logsum = top + jnp.log(total)

    def value_step(block_index, accum):
        key_heads, value_heads, key_spots, key_docs = key_block(
            keys_all, values_all, docs_all, block_index, row_count
        )
        masked = masked_scores(query_heads, key_heads, query_spots, key_spots, query_docs, key_docs)
        probs = jnp.exp(masked - logsum[..., None]).astype(jnp.bfloat16)
        return accum + jnp.einsum(
            "hqk,khd->qhd", probs, value_heads, preferred_element_type=jnp.float32
        )

    accum = lax.fori_loop(
        0, cut_index + 1, value_step, jnp.zeros((row_count, head_count, 64), jnp.float32)
    )
    return (accum.reshape(row_count, -1).astype(jnp.bfloat16), logsum)


def local(
    tokens,
    cotangent,
    segments,
    expert_ids,
    slot_ids,
    kept_mask,
    norm1_gain,
    w_query,
    w_key,
    w_value,
    w_output,
    norm2_gain,
    dense_in,
    dense_out,
    router,
    mixer,
    expert_in,
    expert_out,
):
    micro_count = tokens.shape[1]
    row_count = tokens.shape[2]
    features = tokens.shape[3]
    cut_count = lax.axis_size("cuts")
    cut_index = lax.axis_index("cuts")
    expert_count = router.shape[1]
    capacity = max(2, row_count * 5 // (4 * expert_count))
    gain_one = norm1_gain.astype(jnp.float32)
    gain_two = norm2_gain.astype(jnp.float32)
    router_f = router.astype(jnp.float32)
    mixer_f = mixer.astype(jnp.float32)
    hidden_in = expert_in[0]
    hidden_out = expert_out[0]
    columns = jnp.arange(expert_count * capacity, dtype=jnp.int32)
    expert_range = jnp.arange(expert_count, dtype=jnp.int32)
    acc_gain_one = jnp.zeros_like(gain_one)
    acc_gain_two = jnp.zeros_like(gain_two)
    acc_query = jnp.zeros(w_query.shape, jnp.float32)
    acc_key = jnp.zeros(w_key.shape, jnp.float32)
    acc_value = jnp.zeros(w_value.shape, jnp.float32)
    acc_output = jnp.zeros(w_output.shape, jnp.float32)
    acc_dense_in = jnp.zeros(dense_in.shape, jnp.float32)
    acc_dense_out = jnp.zeros(dense_out.shape, jnp.float32)
    acc_router = jnp.zeros(router.shape, jnp.float32)
    acc_mixer = jnp.zeros(mixer.shape, jnp.float32)
    acc_hidden_in = jnp.zeros(hidden_in.shape, jnp.float32)
    acc_hidden_out = jnp.zeros(hidden_out.shape, jnp.float32)
    results = []
    input_grads = []
    for step_index in range(micro_count):
        x_rows = tokens[0, step_index].astype(jnp.float32)
        docs_all = segments[0, step_index]
        h_one = layer_norm(x_rows, gain_one).astype(jnp.bfloat16)
        query = plain_dot(h_one, w_query).astype(jnp.bfloat16)
        key_rows = plain_dot(h_one, w_key).astype(jnp.bfloat16)
        value_rows = plain_dot(h_one, w_value).astype(jnp.bfloat16)
        keys_all, values_all = (
            lax.all_gather(key_rows, "cuts", axis=0, tiled=True),
            lax.all_gather(value_rows, "cuts", axis=0, tiled=True),
        )
        attended, logsum = attend_forward(
            query, keys_all, values_all, docs_all, cut_index, row_count
        )
        x_two = x_rows + plain_dot(attended, w_output)
        h_two = layer_norm(x_two, gain_two).astype(jnp.bfloat16)
        h_two_f = h_two.astype(jnp.float32)
        pre_dense = plain_dot(h_two, dense_in)
        hidden = gelu_exact(pre_dense).astype(jnp.bfloat16)
        dense_rows = plain_dot(hidden, dense_out)
        chosen = expert_ids[0, step_index]
        kept_int = kept_mask[0, step_index]
        table = jnp.where(
            ((chosen * capacity + slot_ids[0, step_index])[:, None] == columns[None, :])
            & (kept_int[:, None] == 1),
            1.0,
            0.0,
        ).astype(jnp.bfloat16)
        sent = lead_dot(table, h_two).astype(jnp.bfloat16).reshape(expert_count, capacity, features)
        arrived = lax.all_to_all(sent, "expert", split_axis=0, concat_axis=0, tiled=True)
        group_rows = lax.all_gather(arrived, "cuts", axis=0, tiled=True).reshape(-1, features)
        expert_pre = plain_dot(group_rows, hidden_in)
        inner = gelu_exact(expert_pre).astype(jnp.bfloat16)
        partial_out = plain_dot(inner, hidden_out).reshape(
            cut_count * expert_count, capacity, features
        )
        summed = lax.psum_scatter(
            partial_out.astype(jnp.bfloat16), "cuts", scatter_dimension=0, tiled=True
        )
        returned = lax.all_to_all(
            summed, "expert", split_axis=0, concat_axis=0, tiled=True
        ).reshape(expert_count * capacity, features)
        from_experts = plain_dot(table, returned)
        hot_mask = chosen[:, None] == expert_range[None, :]
        kept_rows = kept_int.astype(jnp.float32)
        mix_local = partial(mix_rows, hot_mask=hot_mask, kept_rows=kept_rows)
        mixed, mix_back = jax.vjp(
            mix_local, h_two_f, router_f, mixer_f, dense_rows, from_experts, x_two
        )
        results.append(mixed.astype(jnp.bfloat16))
        grad_y = cotangent[0, step_index].astype(jnp.float32)
        d_h_two, d_router, d_mixer, d_dense, d_from, d_x_two = mix_back(grad_y)
        acc_router = acc_router + d_router
        acc_mixer = acc_mixer + d_mixer
        grad_sent = (
            lead_dot(table, d_from.astype(jnp.bfloat16))
            .astype(jnp.bfloat16)
            .reshape(expert_count, capacity, features)
        )
        grad_arrived = lax.all_to_all(grad_sent, "expert", split_axis=0, concat_axis=0, tiled=True)
        grad_group = lax.all_gather(grad_arrived, "cuts", axis=0, tiled=True).reshape(-1, features)
        d_inner = tail_dot(grad_group, hidden_out)
        acc_hidden_out = acc_hidden_out + lead_dot(inner, grad_group)
        d_expert_pre = gelu_grad(expert_pre, d_inner).astype(jnp.bfloat16)
        acc_hidden_in = acc_hidden_in + lead_dot(group_rows, d_expert_pre)
        d_group = tail_dot(d_expert_pre, hidden_in).reshape(
            cut_count * expert_count, capacity, features
        )
        d_sent = lax.psum_scatter(
            d_group.astype(jnp.bfloat16), "cuts", scatter_dimension=0, tiled=True
        )
        d_back = lax.all_to_all(d_sent, "expert", split_axis=0, concat_axis=0, tiled=True).reshape(
            expert_count * capacity, features
        )
        grad_dense = d_dense.astype(jnp.bfloat16)
        d_hidden = tail_dot(grad_dense, dense_out)
        acc_dense_out = acc_dense_out + lead_dot(hidden, grad_dense)
        d_pre = gelu_grad(pre_dense, d_hidden).astype(jnp.bfloat16)
        acc_dense_in = acc_dense_in + lead_dot(h_two, d_pre)
        d_h_two = d_h_two + tail_dot(d_pre, dense_in) + plain_dot(table, d_back)
        norm_back_two = jax.vjp(layer_norm, x_two, gain_two)[1]
        d_x_norm, d_gain_two = norm_back_two(d_h_two)
        acc_gain_two = acc_gain_two + d_gain_two
        d_x_two = d_x_two + d_x_norm
        grad_att = d_x_two.astype(jnp.bfloat16)
        acc_output = acc_output + lead_dot(attended, grad_att)
        d_att = tail_dot(grad_att, w_output).astype(jnp.bfloat16)
        query_heads = split_heads(query)
        back_heads = split_heads(d_att)
        head_count = query_heads.shape[1]
        query_spots = cut_index * row_count + jnp.arange(row_count, dtype=jnp.int32)
        query_docs = lax.dynamic_slice_in_dim(docs_all, cut_index * row_count, row_count, 0)

        def delta_step(block_index, delta):
            key_heads, value_heads, key_spots, key_docs = key_block(
                keys_all, values_all, docs_all, block_index, row_count
            )
            probs, dprobs = probs_pair(
                query_heads,
                back_heads,
                logsum,
                key_heads,
                value_heads,
                query_spots,
                key_spots,
                query_docs,
                key_docs,
            )
            return delta + jnp.sum(probs * dprobs, axis=-1)

        delta = lax.fori_loop(
            0, cut_index + 1, delta_step, jnp.zeros((head_count, row_count), jnp.float32)
        )

        def grad_step(block_index, carry):
            query_grad, terms = carry
            key_heads, value_heads, key_spots, key_docs = key_block(
                keys_all, values_all, docs_all, block_index, row_count
            )
            probs, dprobs = probs_pair(
                query_heads,
                back_heads,
                logsum,
                key_heads,
                value_heads,
                query_spots,
                key_spots,
                query_docs,
                key_docs,
            )
            score_grad = score_grads(probs, dprobs, delta)
            query_grad = (
                query_grad
                + jnp.einsum(
                    "hqk,khd->qhd", score_grad, key_heads, preferred_element_type=jnp.float32
                )
                * score_scale
            )
            key_grad = (
                jnp.einsum(
                    "hqk,qhd->khd", score_grad, query_heads, preferred_element_type=jnp.float32
                )
                * score_scale
            )
            value_grad = jnp.einsum(
                "hqk,qhd->khd",
                probs.astype(jnp.bfloat16),
                back_heads,
                preferred_element_type=jnp.float32,
            )
            piece = jnp.concatenate(
                [key_grad.reshape(row_count, -1), value_grad.reshape(row_count, -1)], axis=1
            )
            return (
                query_grad,
                lax.dynamic_update_slice_in_dim(terms, piece, block_index * row_count, 0),
            )

        start_terms = jnp.zeros((cut_count * row_count, 2 * features), jnp.float32)
        query_grad, terms = lax.fori_loop(
            0,
            cut_index + 1,
            grad_step,
            (jnp.zeros((row_count, head_count, 64), jnp.float32), start_terms),
        )
        summed_terms = lax.psum_scatter(
            terms.astype(jnp.bfloat16), "cuts", scatter_dimension=0, tiled=True
        ).astype(jnp.float32)
        key_grad = summed_terms[:, :features]
        value_grad = summed_terms[:, features:]
        query_low = query_grad.reshape(row_count, features).astype(jnp.bfloat16)
        key_low = key_grad.astype(jnp.bfloat16)
        value_low = value_grad.astype(jnp.bfloat16)
        acc_query = acc_query + lead_dot(h_one, query_low)
        acc_key = acc_key + lead_dot(h_one, key_low)
        acc_value = acc_value + lead_dot(h_one, value_low)
        d_h_one = (
            tail_dot(query_low, w_query) + tail_dot(key_low, w_key) + tail_dot(value_low, w_value)
        )
        norm_back_one = jax.vjp(layer_norm, x_rows, gain_one)[1]
        d_x_norm_one, d_gain_one = norm_back_one(d_h_one)
        acc_gain_one = acc_gain_one + d_gain_one
        input_grads.append(d_x_two + d_x_norm_one)
    shared = (
        lax.psum_scatter(acc_gain_one, ("expert", "cuts"), scatter_dimension=0, tiled=True),
        lax.psum_scatter(acc_query, ("expert", "cuts"), scatter_dimension=0, tiled=True),
        lax.psum_scatter(acc_key, ("expert", "cuts"), scatter_dimension=0, tiled=True),
        lax.psum_scatter(acc_value, ("expert", "cuts"), scatter_dimension=0, tiled=True),
        lax.psum_scatter(acc_output, ("expert", "cuts"), scatter_dimension=0, tiled=True),
        lax.psum_scatter(acc_gain_two, ("expert", "cuts"), scatter_dimension=0, tiled=True),
        lax.psum_scatter(acc_dense_in, ("expert", "cuts"), scatter_dimension=0, tiled=True),
        lax.psum_scatter(acc_dense_out, ("expert", "cuts"), scatter_dimension=0, tiled=True),
        lax.psum_scatter(acc_router, ("expert", "cuts"), scatter_dimension=0, tiled=True),
        lax.psum_scatter(acc_mixer, ("expert", "cuts"), scatter_dimension=0, tiled=True),
    )
    output = jnp.stack(results)[None]
    grad_tokens = jnp.stack(input_grads)[None]
    return (
        output,
        grad_tokens,
        shared[0],
        shared[1],
        shared[2],
        shared[3],
        shared[4],
        shared[5],
        shared[6],
        shared[7],
        shared[8],
        shared[9],
        acc_hidden_in[None],
        acc_hidden_out[None],
    )


def solution(mesh):
    in_specs = (
        P("expert", None, "cuts", None),
        P("expert", None, "cuts", None),
        P("expert", None, None),
        P("expert", None, "cuts"),
        P("expert", None, "cuts"),
        P("expert", None, "cuts"),
        P(),
        P(),
        P(),
        P(),
        P(),
        P(),
        P(),
        P(),
        P(),
        P(),
        P("expert", None, "cuts"),
        P("expert", "cuts", None),
    )
    out_specs = (
        P("expert", None, "cuts", None),
        P("expert", None, "cuts", None),
        P(("expert", "cuts")),
        P(("expert", "cuts"), None),
        P(("expert", "cuts"), None),
        P(("expert", "cuts"), None),
        P(("expert", "cuts"), None),
        P(("expert", "cuts")),
        P(("expert", "cuts"), None),
        P(("expert", "cuts"), None),
        P(("expert", "cuts"), None),
        P(("expert", "cuts"), None),
        P("expert", None, "cuts"),
        P("expert", "cuts", None),
    )
    return jax.shard_map(local, mesh=mesh, in_specs=in_specs, out_specs=out_specs, check_vma=False)
```

profile of v0, /device:TPU:0, one launch (start us, length us, event | category | flops | bytes accessed | tf_op | source)
XLA Modules:
  0.0 1922.4 jit_solution(18332429958657522441)
XLA Ops:
  27.4 18.2 all-gather.11.cloned.1.call-done
  51.3 25.1 %all-gather.9.cloned.1.call-done = bf16[1024,1024]{1,0:T(8,128)(2,1)} async-done(((bf16[128,1024]{1,0:T(8,128)(2,1)}), bf16[1024,1024]{1,0:T(8,128)(2,1)}) %all-gather.9.cloned.1.call-update) | async-done | bytes 2097168 | tf_op jit(solution)/shard_map/all_gather | solution.py:211
  88.5 18.1 all-gather.17.cloned.1.call-done
  112.3 25.0 %all-gather.15.cloned.1.call-done = bf16[1024,1024]{1,0:T(8,128)(2,1)} async-done(((bf16[128,1024]{1,0:T(8,128)(2,1)}), bf16[1024,1024]{1,0:T(8,128)(2,1)}) %all-gather.15.cloned.1.call-update) | async-done | bytes 2097168 | tf_op jit(solution)/shard_map/all_gather | solution.py:211
  168.6 46.6 %all-gather.19.cloned.1.call-done = bf16[32,40,1024]{2,1,0:T(8,128)(2,1)} async-done(((bf16[4,40,1024]{2,1,0:T(8,128)(2,1)}), bf16[32,40,1024]{2,1,0:T(8,128)(2,1)}) %all-gather.19.cloned.1.call-update) | async-done | bytes 2621456 | tf_op jit(solution)/shard_map/all_gather | solution.py:232
  215.1 10.1 multiply_convert_fusion
  230.5 19.0 all-gather.13.cloned.1.call-done
  249.5 10.1 multiply_convert_fusion.1
  292.5 34.7 %reduce-scatter.23.cloned.1.call-done = bf16[4,40,1024]{2,1,0:T(8,128)(2,1)} async-done(((bf16[32,40,1024]{2,1,0:T(8,128)(2,1)}), bf16[4,40,1024]{2,1,0:T(8,128)(2,1)}) %reduce-scatter.23.cloned.1.call-update) | async-done | bytes 327696 | tf_op jit(solution)/shard_map/reduce_scatter | solution.py:238
  365.2 19.8 %all-gather.21.cloned.1.call-done = bf16[32,40,1024]{2,1,0:T(8,128)(2,1)} async-done(((bf16[4,40,1024]{2,1,0:T(8,128)(2,1)}), bf16[32,40,1024]{2,1,0:T(8,128)(2,1)}) %all-gather.21.cloned.1.call-update) | async-done | bytes 2621456 | tf_op jit(solution)/shard_map/all_gather | solution.py:262
  396.8 22.6 %all-gather.23.cloned.1.call-done = bf16[32,40,1024]{2,1,0:T(8,128)(2,1)} async-done(((bf16[4,40,1024]{2,1,0:T(8,128)(2,1)}), bf16[32,40,1024]{2,1,0:T(8,128)(2,1)}) %all-gather.23.cloned.1.call-update) | async-done | bytes 2621456 | tf_op jit(solution)/shard_map/all_gather | solution.py:262
  467.1 29.8 %reduce-scatter.29.cloned.1.call-done = bf16[4,40,1024]{2,1,0:T(8,128)(2,1)} async-done(((bf16[32,40,1024]{2,1,0:T(8,128)(2,1)}), bf16[4,40,1024]{2,1,0:T(8,128)(2,1)}) %reduce-scatter.29.cloned.1.call-update) | async-done | bytes 327696 | tf_op jit(solution)/shard_map/reduce_scatter | solution.py:270
  563.0 71.4 %reduce-scatter.43.cloned.1.call-done = bf16[128,2048]{1,0:T(8,128)(2,1)} async-done(((bf16[1024,2048]{1,0:T(8,128)(2,1)}), bf16[128,2048]{1,0:T(8,128)(2,1)}) %reduce-scatter.43.cloned.1.call-update) | async-done | bytes 524304
  638.1 67.4 %reduce-scatter.45.cloned.1.call-done = bf16[128,2048]{1,0:T(8,128)(2,1)} async-done(((bf16[1024,2048]{1,0:T(8,128)(2,1)}), bf16[128,2048]{1,0:T(8,128)(2,1)}) %reduce-scatter.45.cloned.1.call-update) | async-done | bytes 524304
  736.8 13.4 convolution_add_fusion
  750.3 90.1 %reduce-scatter.49.cloned.1.call-done = f32[32,2]{1,0:T(8,128)} async-done(((f32[1024,2]{1,0:T(8,128)}), f32[32,2]{1,0:T(8,128)}) %reduce-scatter.49.cloned.1.call-update) | async-done | bytes 272
  841.7 131.6 %reduce-scatter.47.cloned.1.call-done = f32[32,4]{1,0:T(8,128)} async-done(((f32[1024,4]{1,0:T(8,128)}), f32[32,4]{1,0:T(8,128)}) %reduce-scatter.47.cloned.1.call-update) | async-done | bytes 528
  995.3 37.4 %all-reduce.6 = (f32[1024]{0:T(1024)S(1)}, f32[1024]{0:T(1024)S(1)}) all-reduce(f32[1024]{0:T(1024)S(1)} %add.420, f32[1024]{0:T(1024)S(1)} %add.425), channel_id=8, replica_groups=mesh['expert'=4,'cuts'=8] {'expert','cuts'}, use_global_device_ids=true, to_apply=%region_72.73.clone | all-reduce | flops 2048 | bytes 16384
  1037.1 78.0 %reduce-scatter.31.cloned.1.call-done = f32[32,1024]{1,0:T(8,128)} async-done(((f32[1024,1024]{1,0:T(8,128)}), f32[32,1024]{1,0:T(8,128)}) %reduce-scatter.31.cloned.1.call-update) | async-done | bytes 131088 | tf_op jit(solution)/shard_map/reduce_scatter | solution.py:387
  1115.1 142.2 %reduce-scatter.37.cloned.1.call-done = f32[32,1024]{1,0:T(8,128)} async-done(((f32[1024,1024]{1,0:T(8,128)}), f32[32,1024]{1,0:T(8,128)}) %reduce-scatter.37.cloned.1.call-update) | async-done | bytes 131088 | tf_op jit(solution)/shard_map/reduce_scatter | solution.py:390
  1257.3 142.3 %reduce-scatter.33.cloned.1.call-done = f32[32,1024]{1,0:T(8,128)} async-done(((f32[1024,1024]{1,0:T(8,128)}), f32[32,1024]{1,0:T(8,128)}) %reduce-scatter.33.cloned.1.call-update) | async-done | bytes 131088 | tf_op jit(solution)/shard_map/reduce_scatter | solution.py:388
  1399.6 142.3 %reduce-scatter.35.cloned.1.call-done = f32[32,1024]{1,0:T(8,128)} async-done(((f32[1024,1024]{1,0:T(8,128)}), f32[32,1024]{1,0:T(8,128)}) %reduce-scatter.35.cloned.1.call-update) | async-done | bytes 131088 | tf_op jit(solution)/shard_map/reduce_scatter | solution.py:389
  1541.9 186.2 %reduce-scatter.39.cloned.1.call-done = f32[32,4096]{1,0:T(8,128)} async-done(((f32[1024,4096]{1,0:T(8,128)}), f32[32,4096]{1,0:T(8,128)}) %reduce-scatter.39.cloned.1.call-update) | async-done | bytes 524304 | tf_op jit(solution)/shard_map/reduce_scatter | solution.py:392
  1728.1 187.3 %reduce-scatter.41.cloned.1.call-done = f32[128,1024]{1,0:T(8,128)} async-done(((f32[4096,1024]{1,0:T(8,128)}), f32[128,1024]{1,0:T(8,128)}) %reduce-scatter.41.cloned.1.call-update) | async-done | bytes 524304 | tf_op jit(solution)/shard_map/reduce_scatter | solution.py:393
  (551 shorter events, 363.9 us)
Async XLA Ops:
  7.2 38.4 %all-gather.11.cloned.1.call-start = ((), (), s32[]{:S(2)}) async-start(), calls=%async_computation.23 | async-start | bytes 2359296 | tf_op jit(solution)/shard_map/all_gather | solution.py:210
  13.6 62.8 %all-gather.9.cloned.1.call-start = ((), (), s32[]{:S(2)}) async-start(), calls=%async_computation.22 | async-start | bytes 2359296 | tf_op jit(solution)/shard_map/all_gather | solution.py:211
  16.5 90.1 %all-gather.17.cloned.1.call-start = ((), (), s32[]{:S(2)}) async-start(), calls=%async_computation.27 | async-start | bytes 2359296 | tf_op jit(solution)/shard_map/all_gather | solution.py:210
  19.4 118.0 %all-gather.15.cloned.1.call-start = ((), (), s32[]{:S(2)}) async-start(), calls=%async_computation.26 | async-start | bytes 2359296 | tf_op jit(solution)/shard_map/all_gather | solution.py:211
  22.2 192.9 %all-gather.19.cloned.1.call-start = ((), (), s32[]{:S(2)}) async-start(), calls=%async_computation.28 | async-start | bytes 2949120 | tf_op jit(solution)/shard_map/all_gather | solution.py:232
  158.5 91.0 %all-gather.13.cloned.1.call-start = ((), (), s32[]{:S(2)}) async-start(), calls=%async_computation.24 | async-start | bytes 2949120 | tf_op jit(solution)/shard_map/all_gather | solution.py:232
  168.3 120.0 %reduce-scatter.25.cloned.1.call-start = ((), (), s32[]{:S(2)}) async-start(), calls=%async_computation.29 | async-start | bytes 2949120 | tf_op jit(solution)/shard_map/reduce_scatter | solution.py:238
  229.5 97.7 %reduce-scatter.23.cloned.1.call-start = ((), (), s32[]{:S(2)}) async-start(), calls=%async_computation.25 | async-start | bytes 2949120 | tf_op jit(solution)/shard_map/reduce_scatter | solution.py:238
  288.3 38.9 %all-to-all-start.3 = ((bf16[4,40,1024]{2,1,0:T(8,128)(2,1)}), bf16[4,40,1024]{2,1,0:T(8,128)(2,1)}, u32[]{:S(2)}, u32[]{:S(2)}) async-start(bf16[4,40,1024]{2,1,0:T(8,128)(2,1)} %reduce-scatter.25.cloned.1.call-done), calls=%async_computation.5 | async-start | bytes 655360 | tf_op jit(solution)/shard_map/all_to_all | solution.py:241
  331.3 53.7 %all-gather.21.cloned.1.call-start = ((), (), s32[]{:S(2)}) async-start(), calls=%async_computation.30 | async-start | bytes 2949120 | tf_op jit(solution)/shard_map/all_gather | solution.py:262
  354.0 65.4 %all-gather.23.cloned.1.call-start = ((), (), s32[]{:S(2)}) async-start(), calls=%async_computation.32 | async-start | bytes 2949120 | tf_op jit(solution)/shard_map/all_gather | solution.py:262
  364.7 96.9 %reduce-scatter.27.cloned.1.call-start = ((), (), s32[]{:S(2)}) async-start(), calls=%async_computation.31 | async-start | bytes 2949120 | tf_op jit(solution)/shard_map/reduce_scatter | solution.py:270
  395.2 101.7 %reduce-scatter.29.cloned.1.call-start = ((), (), s32[]{:S(2)}) async-start(), calls=%async_computation.33 | async-start | bytes 2949120 | tf_op jit(solution)/shard_map/reduce_scatter | solution.py:270
  461.6 35.3 %all-to-all-start.5 = ((bf16[4,40,1024]{2,1,0:T(8,128)(2,1)}), bf16[4,40,1024]{2,1,0:T(8,128)(2,1)}, u32[]{:S(2)}, u32[]{:S(2)}) async-start(bf16[4,40,1024]{2,1,0:T(8,128)(2,1)} %reduce-scatter.27.cloned.1.call-done), calls=%async_computation.8 | async-start | bytes 655360 | tf_op jit(solution)/shard_map/all_to_all | solution.py:273
  501.0 133.4 %reduce-scatter.43.cloned.1.call-start = ((), (), s32[]{:S(2)}) async-start(), calls=%async_computation.40 | async-start | bytes 4718592
  532.6 173.0 %reduce-scatter.45.cloned.1.call-start = ((), (), s32[]{:S(2)}) async-start(), calls=%async_computation.41 | async-start | bytes 4718592
  550.3 290.1 %reduce-scatter.49.cloned.1.call-start = ((), (), s32[]{:S(2)}) async-start(), calls=%async_computation.43 | async-start | bytes 540672
  552.7 420.6 %reduce-scatter.47.cloned.1.call-start = ((), (), s32[]{:S(2)}) async-start(), calls=%async_computation.42 | async-start | bytes 540672
  554.0 561.0 %reduce-scatter.31.cloned.1.call-start = ((), (), s32[]{:S(2)}) async-start(), calls=%async_computation.34 | async-start | bytes 4325376 | tf_op jit(solution)/shard_map/reduce_scatter | solution.py:387
  558.6 698.7 %reduce-scatter.37.cloned.1.call-start = ((), (), s32[]{:S(2)}) async-start(), calls=%async_computation.37 | async-start | bytes 4325376 | tf_op jit(solution)/shard_map/reduce_scatter | solution.py:390
  563.0 836.6 %reduce-scatter.33.cloned.1.call-start = ((), (), s32[]{:S(2)}) async-start(), calls=%async_computation.35 | async-start | bytes 4325376 | tf_op jit(solution)/shard_map/reduce_scatter | solution.py:388
  710.6 831.3 %reduce-scatter.35.cloned.1.call-start = ((), (), s32[]{:S(2)}) async-start(), calls=%async_computation.36 | async-start | bytes 4325376 | tf_op jit(solution)/shard_map/reduce_scatter | solution.py:389
  715.4 1012.7 %reduce-scatter.39.cloned.1.call-start = ((), (), s32[]{:S(2)}) async-start(), calls=%async_computation.38 | async-start | bytes 17301504 | tf_op jit(solution)/shard_map/reduce_scatter | solution.py:392
  727.3 1188.1 %reduce-scatter.41.cloned.1.call-start = ((), (), s32[]{:S(2)}) async-start(), calls=%async_computation.39 | async-start | bytes 17301504 | tf_op jit(solution)/shard_map/reduce_scatter | solution.py:393
  (131 other events, 2373.5 us)
Sparse Core Ops, SparseCore 0:
  13.7 31.7 all-gather.10
  47.7 28.5 all-gather.8
  78.0 28.5 all-gather.16
  108.6 28.7 all-gather.14
  158.7 56.4 all-gather.18
  216.6 32.8 all-gather.12
  251.8 36.4 reduce-scatter.24
  290.6 36.5 reduce-scatter.22
  354.1 30.8 all-gather.20
  386.5 32.8 all-gather.22
  421.7 36.4 reduce-scatter.26
  460.3 36.5 reduce-scatter.28
  532.7 101.6 reduce-scatter.42
  636.6 68.9 reduce-scatter.44
  708.2 132.1 reduce-scatter.48
  843.1 130.1 reduce-scatter.46
  976.0 138.9 reduce-scatter.30
  1117.8 139.4 reduce-scatter.36
  1260.1 139.3 reduce-scatter.32
  1402.2 139.5 reduce-scatter.34
  1544.8 183.2 reduce-scatter.38
  1731.0 184.3 reduce-scatter.40
where the time goes:
time: 1930 us; the launch traced here: 1920 us
  waiting for transfers between devices  1510 us (78%)
  matrix products  216 us (11%)
  blocking collectives  75.2 us (4%)
  local copies, waits for them, and re-layouts  73.7 us (4%)
    unnamed x26, waiting for transfers between devices  361 us
    reduce_scatter x1, waiting for transfers between devices, local(): lax.psum_scatter(acc_dense_out, ('expert', 'cuts'), scatter_dimension=0,...  187 us
    reduce_scatter x1, waiting for transfers between devices, local(): lax.psum_scatter(acc_dense_in, ('expert', 'cuts'), scatter_dimension=0, t...  186 us
    reduce_scatter x1, waiting for transfers between devices, local(): lax.psum_scatter(acc_value, ('expert', 'cuts'), scatter_dimension=0, tile...  142 us
    reduce_scatter x1, waiting for transfers between devices, local(): lax.psum_scatter(acc_key, ('expert', 'cuts'), scatter_dimension=0, tiled=...  142 us
    reduce_scatter x1, waiting for transfers between devices, local(): lax.psum_scatter(acc_output, ('expert', 'cuts'), scatter_dimension=0, til...  142 us
    reduce_scatter x1, waiting for transfers between devices, local(): lax.psum_scatter(acc_query, ('expert', 'cuts'), scatter_dimension=0, tile...  78 us
    dot_general x20, matrix products, plain_dot(): return jnp.dot(left, right, preferred_element_type=jnp.float32)  74.9 us
  transfers between devices with their start and end apart: 26, of which 23 were waited for; matrix products, arithmetic and copies ran while one was open for 12% of the time, Pallas kernels for 0%

commit v1 on v0

v1 whole, which is shorter than its diff:
```python
from functools import partial

import jax
import jax.numpy as jnp
from jax import lax
from jax.experimental import pallas as pl
from jax.experimental.pallas import tpu as pltpu
from jax.sharding import PartitionSpec as P

MESH = pl.DeviceIdType.MESH
score_scale = 0.125
masked_value = -1e30
norm_eps = 1e-05


def softmax_rows(values):
    raised = jnp.exp(values - jnp.max(values, axis=-1, keepdims=True))
    return raised / jnp.sum(raised, axis=-1, keepdims=True)


def plain_dot(left, right):
    return jnp.dot(left, right, preferred_element_type=jnp.float32)


def lead_dot(left, right):
    return lax.dot_general(
        left, right, (((0,), (0,)), ((), ())), preferred_element_type=jnp.float32
    )


def tail_dot(left, right):
    return lax.dot_general(
        left, right, (((1,), (1,)), ((), ())), preferred_element_type=jnp.float32
    )


def greet_line(cut_count, every):
    cut = lax.axis_index("cuts")
    group = lax.axis_index("expert")
    barrier = pltpu.get_barrier_semaphore()
    hops = range(1, cut_count) if every else [1] + list(range(2, cut_count, 2))
    for hop in hops:
        pl.semaphore_signal(barrier, inc=1, device_id=(group, jnp.bitwise_xor(cut, hop)), device_id_type=MESH)
    pl.semaphore_wait(barrier, len(hops))


def gather_kernel(chain, x_ref, out_ref, send_sem, recv_sem, pair_send, pair_recv, own_sem):
    micro_count, cut_count = out_ref.shape[0], out_ref.shape[1]
    cut = lax.axis_index("cuts")
    group = lax.axis_index("expert")
    sibling = jnp.bitwise_xor(cut, 1)
    level, side = cut // 2, cut % 2
    levels = cut_count // 2
    greet_line(cut_count, False)

    def copy_to(m, src, source, target, ssem, rsem):
        return pltpu.make_async_remote_copy(
            src_ref=src, dst_ref=out_ref.at[m, source], send_sem=ssem, recv_sem=rsem,
            device_id=(group, target), device_id_type=MESH)

    own = []
    for m in range(micro_count):
        c = pltpu.make_async_copy(x_ref.at[m], out_ref.at[m, cut], own_sem.at[m])
        c.start()
        own.append(c)
    if chain:
        def hop(m, step, up, start):
            source = cut - 2 * step if up else cut + 2 * step
            target = cut + 2 if up else cut - 2
            ok = (level - step >= 0) & (level + 1 < levels) if up else (level + step < levels) & (level - 1 >= 0)
            src = x_ref.at[m] if step == 0 else out_ref.at[m, source]
            @pl.when(ok)
            def _():
                cp = copy_to(m, src, source, target, send_sem.at[m, step, 0 if up else 1], recv_sem.at[m, step, 0 if up else 1])
                if start:
                    cp.start()
                else:
                    cp.wait_send()
        def arrive(m, step, up):
            source = cut - 2 * (step + 1) if up else cut + 2 * (step + 1)
            ok = (level - step - 1 >= 0) if up else (level + step + 1 < levels)
            @pl.when(ok)
            def _():
                copy_to(m, x_ref.at[m], source, sibling, send_sem.at[m, step, 0 if up else 1], recv_sem.at[m, step, 0 if up else 1]).wait_recv()
            if step + 1 < levels - 1:
                hop(m, step + 1, up, True)
            @pl.when(ok)
            def _():
                copy_to(m, out_ref.at[m, source], source, sibling, pair_send.at[m, source], pair_recv.at[m, source]).start()
        for m in range(micro_count):
            hop(m, 0, True, True)
            hop(m, 0, False, True)
        for m in range(micro_count):
            copy_to(m, x_ref.at[m], cut, sibling, pair_send.at[m, cut], pair_recv.at[m, cut]).start()
        for step in range(levels - 1):
            for m in range(micro_count):
                arrive(m, step, True)
                arrive(m, step, False)
        for step in range(levels - 1):
            for m in range(micro_count):
                hop(m, step, True, False)
                hop(m, step, False, False)
    else:
        hops = list(range(2, cut_count, 2))
        def peer(m, k, hop_):
            return copy_to(m, x_ref.at[m], cut, jnp.bitwise_xor(cut, hop_), send_sem.at[m, k, 0], recv_sem.at[m, k, 0])
        for m in range(micro_count):
            for k, hop_ in enumerate(hops):
                peer(m, k, hop_).start()
            copy_to(m, x_ref.at[m], cut, sibling, pair_send.at[m, cut], pair_recv.at[m, cut]).start()
        for m in range(micro_count):
            for k, hop_ in enumerate(hops):
                source = jnp.bitwise_xor(cut, hop_)
                copy_to(m, x_ref.at[m], source, sibling, send_sem.at[m, k, 0], recv_sem.at[m, k, 0]).wait_recv()
                copy_to(m, out_ref.at[m, source], source, sibling, pair_send.at[m, source], pair_recv.at[m, source]).start()
        for m in range(micro_count):
            for k, hop_ in enumerate(hops):
                peer(m, k, hop_).wait_send()
    for m in range(micro_count):
        own[m].wait()
        for z in range(levels):
            mine = 2 * z + side
            theirs = 2 * z + 1 - side
            copy_to(m, out_ref.at[m, mine], mine, sibling, pair_send.at[m, mine], pair_recv.at[m, theirs]).wait_send()
            copy_to(m, out_ref.at[m, mine], theirs, sibling, pair_send.at[m, mine], pair_recv.at[m, theirs]).wait_recv()


def cut_gather(x, cut_count, call_id, chain=True, space=pltpu.VMEM):
    micro_count, rows, width = x.shape
    levels = cut_count // 2
    return pl.pallas_call(
        partial(gather_kernel, chain),
        out_shape=jax.ShapeDtypeStruct((micro_count, cut_count, rows, width), x.dtype),
        in_specs=[pl.BlockSpec(memory_space=pltpu.VMEM)],
        out_specs=pl.BlockSpec(memory_space=space),
        scratch_shapes=[
            pltpu.SemaphoreType.DMA((micro_count, levels - 1, 2)),
            pltpu.SemaphoreType.DMA((micro_count, levels - 1, 2)),
            pltpu.SemaphoreType.DMA((micro_count, cut_count)),
            pltpu.SemaphoreType.DMA((micro_count, cut_count)),
            pltpu.SemaphoreType.DMA((micro_count,)),
        ],
        compiler_params=pltpu.CompilerParams(collective_id=call_id, has_side_effects=True, vmem_limit_bytes=48 * 2**20),
    )(x)


def scatter_kernel(x_ref, out_ref, pair_buf, comb, far_buf, send_sem, recv_sem, pair_send, pair_recv):
    micro_count, cut_count, rows, width = x_ref.shape
    cut = lax.axis_index("cuts")
    group = lax.axis_index("expert")
    sibling = jnp.bitwise_xor(cut, 1)
    side = cut % 2
    levels = cut_count // 2
    greet_line(cut_count, False)
    hops = [levels - 1 - k for k in range(levels)]

    def pair_copy(m, k):
        dest = jnp.bitwise_xor(cut, 2 * k)
        return pltpu.make_async_remote_copy(
            src_ref=x_ref.at[m, jnp.bitwise_xor(dest, 1)], dst_ref=pair_buf.at[m, k],
            send_sem=pair_send.at[m, k], recv_sem=pair_recv.at[m, k],
            device_id=(group, sibling), device_id_type=MESH)

    def far_copy(m, k):
        return pltpu.make_async_remote_copy(
            src_ref=comb.at[m, k], dst_ref=far_buf.at[m, k],
            send_sem=send_sem.at[m, k], recv_sem=recv_sem.at[m, k],
            device_id=(group, jnp.bitwise_xor(cut, 2 * k)), device_id_type=MESH)

    for m in range(micro_count):
        for k in hops:
            pair_copy(m, k).start()
    for m in range(micro_count):
        for k in hops:
            pair_copy(m, k).wait_recv()
            total = x_ref[m, jnp.bitwise_xor(cut, 2 * k)].astype(jnp.float32) + pair_buf[m, k].astype(jnp.float32)
            if k:
                comb[m, k] = total.astype(comb.dtype)
                far_copy(m, k).start()
            else:
                out_ref[m] = total
    for m in range(micro_count):
        for k in hops:
            if k:
                far_copy(m, k).wait_recv()
                out_ref[m] = out_ref[m] + far_buf[m, k].astype(jnp.float32)
    for m in range(micro_count):
        for k in hops:
            pair_copy(m, k).wait_send()
            if k:
                far_copy(m, k).wait_send()


def cut_scatter(x, call_id):
    micro_count, cut_count, rows, width = x.shape
    levels = cut_count // 2
    return pl.pallas_call(
        scatter_kernel,
        out_shape=jax.ShapeDtypeStruct((micro_count, rows, width), jnp.float32),
        in_specs=[pl.BlockSpec(memory_space=pltpu.VMEM)],
        out_specs=pl.BlockSpec(memory_space=pltpu.VMEM),
        scratch_shapes=[
            pltpu.VMEM((micro_count, levels, rows, width), x.dtype),
            pltpu.VMEM((micro_count, levels, rows, width), x.dtype),
            pltpu.VMEM((micro_count, levels, rows, width), x.dtype),
            pltpu.SemaphoreType.DMA((micro_count, levels)),
            pltpu.SemaphoreType.DMA((micro_count, levels)),
            pltpu.SemaphoreType.DMA((micro_count, levels)),
            pltpu.SemaphoreType.DMA((micro_count, levels)),
        ],
        compiler_params=pltpu.CompilerParams(collective_id=call_id, has_side_effects=True, vmem_limit_bytes=48 * 2**20),
    )(x)


def swap_kernel(to_rows, x_ref, out_ref, send_sem, recv_sem, own_sem):
    micro_count = x_ref.shape[0]
    cut = lax.axis_index("cuts")
    group = lax.axis_index("expert")
    cut_count = max(x_ref.shape[1], out_ref.shape[1]) // min(x_ref.shape[1], out_ref.shape[1])
    rows = min(x_ref.shape[1], out_ref.shape[1])
    width = min(x_ref.shape[2], out_ref.shape[2])
    greet_line(cut_count, True)

    def by_rows(ref, m, who):
        return ref.at[m, pl.ds(pl.multiple_of(who * rows, rows), rows), :]

    def by_columns(ref, m, who):
        return ref.at[m, :, pl.ds(pl.multiple_of(who * width, width), width)]

    def copy(m, hop):
        target = jnp.bitwise_xor(cut, hop)
        src = by_rows(x_ref, m, target) if to_rows else by_columns(x_ref, m, target)
        dst = by_columns(out_ref, m, cut) if to_rows else by_rows(out_ref, m, cut)
        return pltpu.make_async_remote_copy(
            src_ref=src, dst_ref=dst, send_sem=send_sem.at[m, hop], recv_sem=recv_sem.at[m, hop],
            device_id=(group, target), device_id_type=MESH)

    for m in range(micro_count):
        for hop in range(cut_count - 1, 0, -1):
            copy(m, hop).start()
        src = by_rows(x_ref, m, cut) if to_rows else by_columns(x_ref, m, cut)
        dst = by_columns(out_ref, m, cut) if to_rows else by_rows(out_ref, m, cut)
        pltpu.make_async_copy(src, dst, own_sem.at[m]).start()
    for m in range(micro_count):
        for hop in range(cut_count - 1, 0, -1):
            copy(m, hop).wait()
        src = by_rows(x_ref, m, cut) if to_rows else by_columns(x_ref, m, cut)
        dst = by_columns(out_ref, m, cut) if to_rows else by_rows(out_ref, m, cut)
        pltpu.make_async_copy(src, dst, own_sem.at[m]).wait()


def cut_swap(x, cut_count, to_rows, call_id):
    micro_count, rows, width = x.shape
    shape = (micro_count, rows // cut_count, width * cut_count) if to_rows else (micro_count, rows * cut_count, width // cut_count)
    return pl.pallas_call(
        partial(swap_kernel, to_rows),
        out_shape=jax.ShapeDtypeStruct(shape, x.dtype),
        in_specs=[pl.BlockSpec(memory_space=pltpu.VMEM)],
        out_specs=pl.BlockSpec(memory_space=pltpu.VMEM),
        scratch_shapes=[
            pltpu.SemaphoreType.DMA((micro_count, cut_count)),
            pltpu.SemaphoreType.DMA((micro_count, cut_count)),
            pltpu.SemaphoreType.DMA((micro_count,)),
        ],
        compiler_params=pltpu.CompilerParams(collective_id=call_id, has_side_effects=True, vmem_limit_bytes=48 * 2**20),
    )(x)


def head_masks(width, heads):
    lane = lax.broadcasted_iota(jnp.int32, (1, width), 1)
    size = width // heads
    return [((lane >= h * size) & (lane < (h + 1) * size)) for h in range(heads)]


def allowed_mask(first_ref, start, rows, keys):
    query_spots = start + lax.broadcasted_iota(jnp.int32, (rows, keys), 0)
    key_spots = lax.broadcasted_iota(jnp.int32, (rows, keys), 1)
    return (key_spots <= query_spots) & (key_spots >= first_ref[0, pl.ds(start, rows), :])


def attend_kernel(heads, qkv_ref, first_ref, att_ref, lse_ref):
    length, width = att_ref.shape[1], att_ref.shape[2]
    rows = min(256, length)
    masks = head_masks(width, heads)
    for block in range(length // rows):
        start, keys = block * rows, (block + 1) * rows
        allowed = allowed_mask(first_ref, start, rows, keys)
        query = qkv_ref[0, pl.ds(start, rows), 0:width] * jnp.bfloat16(score_scale)
        key = qkv_ref[0, 0:keys, width : 2 * width]
        value = qkv_ref[0, 0:keys, 2 * width : 3 * width]
        att = jnp.zeros((rows, width), jnp.float32)
        logs = jnp.zeros((rows, width), jnp.float32)
        for mask in masks:
            scores = tail_dot(jnp.where(mask, query, jnp.bfloat16(0)), key)
            scores = jnp.where(allowed, scores, masked_value)
            top = jnp.max(scores, axis=-1, keepdims=True)
            raised = jnp.exp(scores - top)
            total = jnp.sum(raised, axis=-1, keepdims=True)
            probs = (raised * (1.0 / total)).astype(jnp.bfloat16)
            att = jnp.where(mask, plain_dot(probs, value), att)
            logs = jnp.where(mask, top + jnp.log(total), logs)
        att_ref[0, pl.ds(start, rows), :] = att.astype(jnp.bfloat16)
        lse_ref[0, pl.ds(start, rows), :] = logs


def attend(qkv, first, heads):
    micro_count, length, width = qkv.shape
    width = width // 3
    block = lambda w: pl.BlockSpec((1, length, w), lambda m: (m, 0, 0))
    return pl.pallas_call(
        partial(attend_kernel, heads),
        grid=(micro_count,),
        out_shape=(
            jax.ShapeDtypeStruct((micro_count, length, width), jnp.bfloat16),
            jax.ShapeDtypeStruct((micro_count, length, width), jnp.float32),
        ),
        in_specs=[block(3 * width), block(1)],
        out_specs=(block(width), block(width)),
        compiler_params=pltpu.CompilerParams(vmem_limit_bytes=48 * 2**20),
    )(qkv, first)


def attend_back_kernel(heads, qkv_ref, first_ref, lse_ref, back_ref, out_ref, key_acc, value_acc):
    length, width = back_ref.shape[1], back_ref.shape[2]
    rows = min(256, length)
    masks = head_masks(width, heads)
    key_acc[...] = jnp.zeros_like(key_acc)
    value_acc[...] = jnp.zeros_like(value_acc)
    zero = jnp.bfloat16(0)
    for block in range(length // rows):
        start, keys = block * rows, (block + 1) * rows
        allowed = allowed_mask(first_ref, start, rows, keys)
        query = qkv_ref[0, pl.ds(start, rows), 0:width] * jnp.bfloat16(score_scale)
        key = qkv_ref[0, 0:keys, width : 2 * width]
        value = qkv_ref[0, 0:keys, 2 * width : 3 * width]
        back = back_ref[0, pl.ds(start, rows), :]
        logs = lse_ref[0, pl.ds(start, rows), :]
        query_grad = jnp.zeros((rows, width), jnp.float32)
        for h, mask in enumerate(masks):
            one_query = jnp.where(mask, query, zero)
            one_back = jnp.where(mask, back, zero)
            scores = jnp.where(allowed, tail_dot(one_query, key), masked_value)
            spot = h * (width // heads)
            probs = jnp.exp(scores - logs[:, spot : spot + 1])
            dprobs = tail_dot(one_back, value)
            weighted = probs * dprobs
            delta = jnp.sum(weighted, axis=-1, keepdims=True)
            score_grad = (weighted - probs * delta).astype(jnp.bfloat16)
            query_grad = jnp.where(mask, plain_dot(score_grad, key), query_grad)
            key_acc[0:keys, :] += lead_dot(score_grad, one_query)
            value_acc[0:keys, :] += lead_dot(probs.astype(jnp.bfloat16), one_back)
        out_ref[0, pl.ds(start, rows), 0:width] = (query_grad * score_scale).astype(jnp.bfloat16)
    out_ref[0, :, width : 2 * width] = key_acc[...].astype(jnp.bfloat16)
    out_ref[0, :, 2 * width : 3 * width] = value_acc[...].astype(jnp.bfloat16)


def attend_back(qkv, first, lse, back, heads):
    micro_count, length, width = back.shape
    block = lambda w: pl.BlockSpec((1, length, w), lambda m: (m, 0, 0))
    return pl.pallas_call(
        partial(attend_back_kernel, heads),
        grid=(micro_count,),
        out_shape=jax.ShapeDtypeStruct((micro_count, length, 3 * width), jnp.bfloat16),
        in_specs=[block(3 * width), block(1), block(width), block(width)],
        out_specs=block(3 * width),
        scratch_shapes=[pltpu.VMEM((length, width), jnp.float32), pltpu.VMEM((length, width), jnp.float32)],
        compiler_params=pltpu.CompilerParams(vmem_limit_bytes=48 * 2**20),
    )(qkv, first, lse, back)


def norm_parts(values):
    center = values - jnp.mean(values, axis=-1, keepdims=True)
    spread = jnp.mean(center * center, axis=-1, keepdims=True)
    scale = lax.rsqrt(spread + norm_eps)
    return center * scale, scale


def norm_back(normed, scale, gain, grad):
    inner = grad * gain
    return scale * (
        inner
        - jnp.mean(inner, axis=-1, keepdims=True)
        - normed * jnp.mean(inner * normed, axis=-1, keepdims=True)
    )


def gelu_pair(values):
    phi = 0.5 * (1.0 + lax.erf(values * (0.5**0.5)))
    bell = jnp.exp(-0.5 * values * values) * ((2.0 * jnp.pi) ** -0.5)
    return values * phi, phi + values * bell


def softmax_back(probs, grad):
    return probs * (grad - jnp.sum(probs * grad, axis=-1, keepdims=True))


def local(
    tokens, cotangent, segments, expert_ids, slot_ids, kept_mask, norm1_gain, w_query, w_key, w_value, w_output,
    norm2_gain, dense_in, dense_out, router, mixer, expert_in, expert_out,
):
    micro_count, row_count, features = tokens.shape[1:]
    cut_count = lax.axis_size("cuts")
    group_count = lax.axis_size("expert")
    cut = lax.axis_index("cuts")
    length = cut_count * row_count
    head_width = features // cut_count
    heads = head_width // 64
    expert_count = router.shape[1]
    hidden_count = dense_in.shape[1]
    share = hidden_count // cut_count
    piece = share // group_count
    capacity = max(2, row_count * 5 // (4 * expert_count))
    slots = expert_count * capacity
    gain_one = norm1_gain.astype(jnp.float32)
    gain_two = norm2_gain.astype(jnp.float32)
    f32, low = jnp.float32, jnp.bfloat16

    code = jnp.where(kept_mask[0] == 1, expert_ids[0] * capacity + slot_ids[0], -1)
    codes = lax.all_gather(code, "cuts", axis=1, tiled=True)
    docs = segments[0]
    first = jnp.sum((docs[:, None, :] < docs[:, :, None]).astype(jnp.int32), axis=-1)[..., None]
    grad_all = lax.all_gather(cotangent[0], "cuts", axis=1, tiled=True)
    weights_in = lax.all_gather(expert_in[0], "expert", axis=0)
    weights_out = lax.all_gather(expert_out[0], "expert", axis=0)

    columns = lambda w: lax.dynamic_slice_in_dim(w, cut * head_width, head_width, 1)
    w_qkv = jnp.concatenate([columns(w_query), columns(w_key), columns(w_value)], axis=1)
    own_in = lax.dynamic_index_in_dim(
        dense_in.reshape(features, group_count, cut_count, piece), cut, 2, keepdims=False
    ).reshape(features, share)
    own_out = lax.dynamic_index_in_dim(
        dense_out.reshape(group_count, cut_count, piece, features), cut, 1, keepdims=False
    ).reshape(share, features)

    x_rows = tokens[0].astype(f32)
    norm_one, scale_one = norm_parts(x_rows)
    h_one = (norm_one * gain_one).astype(low)
    h_all = cut_gather(h_one, cut_count, 1).reshape(micro_count, length, features)
    qkv = jnp.einsum("mtf,fk->mtk", h_all, w_qkv, preferred_element_type=f32).astype(low)
    att_part, lse = attend(qkv, first, heads)
    attended = cut_swap(att_part, cut_count, True, 2).reshape(-1, features)
    x_two = x_rows.reshape(-1, features) + plain_dot(attended, w_output)
    norm_two, scale_two = norm_parts(x_two)
    h_two = (norm_two * gain_two).astype(low)
    h2_all = cut_gather(h_two.reshape(micro_count, row_count, features), cut_count, 3).reshape(-1, features)
    g_all = grad_all.reshape(-1, features)
    gy_all = g_all.astype(f32)
    tokens_all = micro_count * length

    code_all = codes.reshape(tokens_all)
    chosen = jnp.where(code_all >= 0, code_all // capacity, -1)
    hot = (chosen[:, None] == jnp.arange(expert_count, dtype=jnp.int32)[None, :]).astype(f32)
    routed = softmax_rows(plain_dot(h2_all, router))
    gate = jnp.sum(hot * routed, axis=-1, keepdims=True)
    mixing = softmax_rows(plain_dot(h2_all, mixer))
    mix_gate = mixing[:, 1:2] * gate

    pre = plain_dot(h2_all, own_in)
    act, slope = gelu_pair(pre)
    hidden = act.astype(low)
    dense_part = plain_dot(hidden, own_out)
    g_dense = (mixing[:, 0:1] * gy_all).astype(low)
    d_pre = (tail_dot(g_dense, own_out) * slope).astype(low)
    d_own_in = lead_dot(h2_all, d_pre)
    d_own_out = lead_dot(hidden, g_dense)

    blocks = tokens_all // row_count
    table = (code_all.reshape(blocks, row_count, 1) == jnp.arange(slots, dtype=jnp.int32)).astype(low)
    to_slots = lambda rows: (
        jnp.einsum("btc,btd->bcd", table, rows.reshape(blocks, row_count, features), preferred_element_type=f32)
        .astype(low)
        .reshape(blocks, expert_count, capacity, features)
        .transpose(1, 0, 2, 3)
        .reshape(expert_count, blocks * capacity, features)
    )
    to_rows = lambda rows: jnp.einsum(
        "btc,bcd->btd",
        table,
        rows.reshape(expert_count, blocks, capacity, features).transpose(1, 0, 2, 3).reshape(blocks, slots, features),
        preferred_element_type=f32,
    ).reshape(tokens_all, features)
    batched = lambda spec, a, b: jnp.einsum(spec, a, b, preferred_element_type=f32)
    sent = to_slots(h2_all)
    g_sent = to_slots((mix_gate * gy_all).astype(low))
    e_pre = batched("etf,efk->etk", sent, weights_in)
    e_act, e_slope = gelu_pair(e_pre)
    inner = e_act.astype(low)
    returned = batched("etk,ekf->etf", inner, weights_out).astype(low)
    d_e_pre = (batched("etf,ekf->etk", g_sent, weights_out) * e_slope).astype(low)
    d_sent = batched("etk,efk->etf", d_e_pre, weights_in).astype(low)
    d_weights_in = batched("etf,etk->efk", sent, d_e_pre).astype(low)
    d_weights_out = batched("etk,etf->ekf", inner, g_sent).astype(low)
    fe_part = to_rows(returned)

    dots = jnp.stack([jnp.sum(gy_all * dense_part, axis=-1), jnp.sum(gy_all * fe_part, axis=-1)], axis=-1)
    dots = lax.psum_scatter(
        dots.reshape(micro_count, length, 2), "cuts", scatter_dimension=1, tiled=True
    ).reshape(-1, 2)
    d_h2_part = (tail_dot(d_pre, own_in) + to_rows(d_sent)).astype(low)
    d_h2 = cut_scatter(d_h2_part.reshape(micro_count, cut_count, row_count, features), 4).reshape(-1, features)
    out_part = (mixing[:, 0:1] * dense_part + mix_gate * fe_part).astype(low)
    out_sum = lax.psum_scatter(
        out_part.reshape(micro_count, length, features), "cuts", scatter_dimension=1, tiled=True
    )
    output = (x_two.reshape(out_sum.shape) + out_sum.astype(f32)).astype(low)

    mine = lambda rows: lax.dynamic_slice_in_dim(
        rows.reshape(micro_count, length, -1), cut * row_count, row_count, 1
    ).reshape(micro_count * row_count, -1)
    gy = cotangent[0].reshape(-1, features).astype(f32)
    own_gate, own_mixing, own_hot, own_routed = mine(gate), mine(mixing), mine(hot), mine(routed)
    d_mixing = jnp.concatenate([dots[:, 0:1], own_gate * dots[:, 1:2]], axis=1)
    d_mixer_logits = softmax_back(own_mixing, d_mixing)
    d_router_logits = softmax_back(own_routed, own_hot * (own_mixing[:, 1:2] * dots[:, 1:2]))
    small = jnp.concatenate([router, mixer], axis=1).astype(f32)
    d_logits = jnp.concatenate([d_router_logits, d_mixer_logits], axis=1)
    d_h2 = d_h2 + lax.dot_general(d_logits, small, (((1,), (1,)), ((), ())), preferred_element_type=f32)
    d_small = lead_dot(h_two.astype(f32), d_logits)
    d_gain_two = jnp.sum(d_h2 * norm_two, axis=0)
    d_x_two = gy + norm_back(norm_two, scale_two, gain_two, d_h2)
    g_att = d_x_two.astype(low)
    d_output = lead_dot(attended, g_att)
    d_att = tail_dot(g_att, w_output).astype(low).reshape(micro_count, row_count, features)
    d_att_part = cut_swap(d_att, cut_count, False, 5)
    d_qkv = attend_back(qkv, first, lse, d_att_part, heads)
    d_w_qkv = lead_dot(h_all.reshape(tokens_all, features), d_qkv.reshape(tokens_all, -1))
    d_h1_part = tail_dot(d_qkv.reshape(tokens_all, -1), w_qkv).astype(low)
    d_h1 = cut_scatter(d_h1_part.reshape(micro_count, cut_count, row_count, features), 6)
    grad_tokens = d_x_two.reshape(d_h1.shape) + norm_back(norm_one, scale_one, gain_one, d_h1)

    rows = features // (group_count * cut_count)
    grad_expert_in = lax.psum_scatter(d_weights_in, "expert", scatter_dimension=0).astype(f32)
    grad_expert_out = lax.psum_scatter(d_weights_out, "expert", scatter_dimension=0).astype(f32)
    grad_dense_out = lax.psum_scatter(d_own_out.astype(low), "expert", scatter_dimension=0, tiled=True).astype(f32)

    def to_owner(part):
        summed = lax.psum_scatter(part.astype(low), "expert", scatter_dimension=0, tiled=True)
        return lax.all_to_all(summed.reshape(cut_count, rows, -1), "cuts", split_axis=0, concat_axis=0)

    grad_dense_in = (
        to_owner(d_own_in).astype(f32)
        .reshape(cut_count, rows, group_count, piece)
        .transpose(1, 2, 0, 3)
        .reshape(rows, hidden_count)
    )
    grad_qkv = to_owner(d_w_qkv).astype(f32).reshape(cut_count, rows, 3, head_width).transpose(2, 1, 0, 3)
    grad_qkv = grad_qkv.reshape(3, rows, features)
    wide = jnp.concatenate([d_output, d_small, d_gain_two[:, None]], axis=1).astype(low)
    wide = wide.reshape(group_count, cut_count, rows, -1).transpose(1, 0, 2, 3)
    wide = lax.psum_scatter(wide, "cuts", scatter_dimension=0)
    wide = lax.psum_scatter(wide, "expert", scatter_dimension=0).astype(f32)
    grad_output = wide[:, :features]
    grad_router = wide[:, features : features + expert_count]
    grad_mixer = wide[:, features + expert_count : -1]
    grad_norm2 = wide[:, -1]

    place = (lax.axis_index("expert") * cut_count + cut) * rows
    own_rows = lambda w: lax.dynamic_slice_in_dim(w, place, rows, 0).astype(f32)
    grad_norm1 = sum(
        jnp.sum(own_rows(w) * grad_qkv[k], axis=-1) for k, w in enumerate((w_query, w_key, w_value))
    ) / own_rows(gain_one)
    return (
        output[None], grad_tokens[None], grad_norm1, grad_qkv[0], grad_qkv[1], grad_qkv[2], grad_output, grad_norm2,
        grad_dense_in, grad_dense_out, grad_router, grad_mixer, grad_expert_in[None], grad_expert_out[None],
    )


def solution(mesh):
    in_specs = (
        P("expert", None, "cuts", None),
        P("expert", None, "cuts", None),
        P("expert", None, None),
        P("expert", None, "cuts"),
        P("expert", None, "cuts"),
        P("expert", None, "cuts"),
        P(),
        P(),
        P(),
        P(),
        P(),
        P(),
        P(),
        P(),
        P(),
        P(),
        P("expert", None, "cuts"),
        P("expert", "cuts", None),
    )
    out_specs = (
        P("expert", None, "cuts", None),
        P("expert", None, "cuts", None),
        P(("expert", "cuts")),
        P(("expert", "cuts"), None),
        P(("expert", "cuts"), None),
        P(("expert", "cuts"), None),
        P(("expert", "cuts"), None),
        P(("expert", "cuts")),
        P(("expert", "cuts"), None),
        P(("expert", "cuts"), None),
        P(("expert", "cuts"), None),
        P(("expert", "cuts"), None),
        P("expert", None, "cuts"),
        P("expert", "cuts", None),
    )
    return jax.shard_map(local, mesh=mesh, in_specs=in_specs, out_specs=out_specs, check_vma=False)
```

time: 1930 us -> 731 us (0.38)
  waiting for transfers between devices: 1510 us -> 202 us
  Pallas kernels: 0 us -> 265 us
  matrix products: 216 us -> 124 us
  blocking collectives: 75.2 us -> 13.4 us
    reduce_scatter x10 -> x4, waiting for transfers between devices: 945 us -> 57.2 us  [the longest x1 49.5 us: local(): lax.psum_scatter(out_part.reshape(micro_count, length, features), 'cuts',...]
    pallas_call x0 -> x8, Pallas kernels: none -> 265 us  [the longest x2 108 us: cut_gather(): pl.pallas_call(partial(gather_kernel, chain), out_shape=jax.ShapeDtypeStr...]
    unnamed x26 -> x17, waiting for transfers between devices: 361 us -> 141 us
    all_gather x8 -> x3, waiting for transfers between devices: 194 us -> 0.02 us  [the longest x1 0.02 us: local(): weights_out = lax.all_gather(expert_out[0], 'expert', axis=0)]
    dot_general x20 -> x5, matrix products: 74.9 us -> 20.7 us  [plain_dot(): return jnp.dot(left, right, preferred_element_type=jnp.float32)]
    dot_general x30 -> x12, matrix products: 19.9 us -> 71.7 us  [the longest x6 45.1 us: local(): jnp.einsum(spec, a, b, preferred_element_type=f32)]
    dot_general x20 -> x5, matrix products: 66.1 us -> 19.9 us  [lead_dot(): lax.dot_general(left, right, (((0,), (0,)), ((), ())), preferred_element_...]
    dot_general x16 -> x4, matrix products: 54.9 us -> 12.1 us  [tail_dot(): lax.dot_general(left, right, (((1,), (1,)), ((), ())), preferred_element_...]
  transfers between devices with their start and end apart: 26 -> 14, of which waited for: 23 -> 6; matrix products, arithmetic and copies ran while one was open for 12% -> 22% of each run, Pallas kernels for 0% -> 37%
where the time goes in v1:
time: 731 us; the launch traced here: 722 us
  Pallas kernels  265 us (36%)
  waiting for transfers between devices  202 us (28%)
  matrix products  124 us (17%)
  local copies, waits for them, and re-layouts  65.1 us (9%)
  other arithmetic  29.1 us (4%)
  between operations  15.3 us (2%)
  blocking collectives  13.4 us (2%)
  starting transfers between devices  7.47 us (1%)
    unnamed x17, waiting for transfers between devices  141 us
    pallas_call x2, Pallas kernels, cut_gather(): pl.pallas_call(partial(gather_kernel, chain), out_shape=jax.ShapeDtypeStr...  108 us
    pallas_call x2, Pallas kernels, cut_scatter(): pl.pallas_call(scatter_kernel, out_shape=jax.ShapeDtypeStruct((micro_coun...  99.8 us
    reduce_scatter x1, waiting for transfers between devices, local(): lax.psum_scatter(out_part.reshape(micro_count, length, features), 'cuts',...  49.5 us
    dot_general x6, matrix products, local(): jnp.einsum(spec, a, b, preferred_element_type=f32)  45.1 us
    pallas_call x2, Pallas kernels, cut_swap(): pl.pallas_call(partial(swap_kernel, to_rows), out_shape=jax.ShapeDtypeStr...  36.1 us
    unnamed x87, local copies, waits for them, and re-layouts  35.1 us
    dot_general x5, matrix products, plain_dot(): return jnp.dot(left, right, preferred_element_type=jnp.float32)  20.7 us
  transfers between devices with their start and end apart: 14, of which 6 were waited for; matrix products, arithmetic and copies ran while one was open for 22% of the time, Pallas kernels for 37%

profile of v1, /device:TPU:0, one launch (start us, length us, event | category | flops | bytes accessed | tf_op | source)
XLA Modules:
  0.0 722.4 jit_solution(13484105097109888699)
XLA Ops:
  13.4 13.4 %all-gather = s32[1,2,1024]{2,1,0:T(2,128)S(1)} all-gather(s32[1,2,128]{2,1,0:T(2,128)S(1)} %compare_select_fusion), channel_id=2, replica_groups=mesh['expert'=4,'cuts'=8] {'cuts'}, dimensions={2}, use_global_device_ids=true | all-gather | bytes 9216 | tf_op jit(solution)/shard_map/all_gather | solution.py:419
  35.3 38.4 %shard_map.281 = bf16[2,8,128,1024]{3,2,1,0:T(8,128)(2,1)S(1)} custom-call(bf16[2,128,1024]{2,1,0:T(8,128)(2,1)S(1)} %copy-done.10), custom_call_target="tpu_custom_call" | custom-call | tf_op jit(solution)/shard_map/pallas_call | solution.py:131
  76.1 8.8 %shard_map.282 = (bf16[2,1024,128]{2,1,0:T(8,128)(2,1)S(1)}, f32[2,1024,128]{2,1,0:T(8,128)S(1)}) custom-call(bf16[2,1024,384]{2,1,0:T(8,128)(2,1)S(1)} %convolution_convert_fusion.7.qkv_ref, s32[2,1024,1]{2,1,0:T(8,128)S(1)} %copy.94.first_ref), custom_call_target="tpu_custom_call" | custom-call | tf_op jit(solution)/shard_map/pallas_call | solution.py:310
  86.0 15.5 %shard_map.283 = bf16[2,128,1024]{2,1,0:T(8,128)(2,1)S(1)} custom-call(bf16[2,1024,128]{2,1,0:T(8,128)(2,1)S(1)} %get-tuple-element.16.x_ref), custom_call_target="tpu_custom_call" | custom-call | tf_op jit(solution)/shard_map/pallas_call | solution.py:255
  107.4 69.8 %shard_map.284 = bf16[2,8,128,1024]{3,2,1,0:T(8,128)(2,1)S(1)} custom-call(bf16[2,128,1024]{2,1,0:T(8,128)(2,1)S(1)} %bitcast.235), custom_call_target="tpu_custom_call" | custom-call | tf_op jit(solution)/shard_map/pallas_call | solution.py:131
  190.9 12.0 %copy.95 = bf16[1024,4096]{0,1:T(8,128)(2,1)} copy(bf16[1024,4096]{1,0:T(8,128)(2,1)} %param.30) | data formatting | bytes 16777216 | tf_op args[12]
  212.1 8.8 %multiply_convert_fusion.1 = (bf16[4,640,512]{2,1,0:T(8,128)(2,1)}, f32[4,640,512]{2,1,0:T(8,128)}) fusion(bf16[4,640,1024]{2,1,0:T(8,128)(2,1)} %bitcast.257, bf16[4,1024,512]{2,1,0:T(8,128)(2,1)} %all-gather.6.cloned.1.call-done), kind=kOutput, calls=%fused_computation.22 | convolution fusion | flops 2690908160 | bytes 17301504 | tf_op jit(solution)/shard_map/etf,efk->etk/dot_general | solution.py:482
  221.0 5.9 convolution_convert_fusion.3
  230.0 11.3 %multiply_reduce_fusion = (f32[16,128]{1,0:T(8,128)S(1)}, f32[16,128,1024]{2,1,0:T(8,128)}, f32[16,128,1024]{2,1,0:T(8,128)}) fusion(bf16[16,128,1024]{2,1,0:T(8,128)(2,1)} %bitcast.247, bf16[16,160,1024]{2,1,0:T(8,128)(2,1)} %bitcast.251, s32[16,128]{1,0:T(8,128)S(1)} %eq.47), kind=kOutput, calls=%fused_computation.11 | convolution fusion | flops 677705728 | bytes 26230784 | tf_op jit(solution)/shard_map/btc,bcd->btd/dot_general | solution.py:476
  241.3 9.6 %fusion = (f32[2048]{0:T(1024)S(1)}, bf16[2048,1024]{1,0:T(8,128)(2,1)}, bf16[2048,1024]{1,0:T(8,128)(2,1)}) fusion(bf16[1,2,1024,1024]{3,2,1,0:T(8,128)(2,1)} %all-gather.10.cloned.1.call-done, f32[16,128,1024]{2,1,0:T(8,128)} %get-tuple-element.131, f32[2048]{0:T(1024)S(1)} %bitcast.282, f32[2048]{0:T(1024)S(1)} %bitcast.285, ...), kind=kOutput, calls=%fused_computation.2 | convolution fusion | flops 2166355968 | bytes 24141824 | tf_op jit(solution)/shard_map/dot_general | solution.py:22
  263.2 8.0 %fusion.11 = bf16[4,640,512]{2,1,0:T(8,128)(2,1)} fusion(f32[4,640,512]{2,1,0:T(8,128)} %get-tuple-element.126, bf16[4,640,1024]{2,1,0:T(8,128)(2,1)S(1)} %bitcast.259, bf16[4,512,1024]{2,1,0:T(8,128)(2,1)S(1)} %copy-done.34), kind=kOutput, calls=%fused_computation.21 | convolution fusion | flops 2697461760 | bytes 17301504 | tf_op jit(solution)/shard_map/etf,ekf->etk/dot_general | solution.py:482
  288.0 50.8 %shard_map.285 = f32[2,128,1024]{2,1,0:T(8,128)S(1)} custom-call(bf16[2,8,128,1024]{3,2,1,0:T(8,128)(2,1)S(1)} %bitcast.239), custom_call_target="tpu_custom_call" | custom-call | tf_op jit(solution)/shard_map/pallas_call | solution.py:197
  359.5 20.6 %shard_map.286.back_ref = bf16[2,1024,128]{2,1,0:T(8,128)(2,1)S(1)} custom-call(bf16[2,128,1024]{2,1,0:T(8,128)(2,1)S(1)} %bitcast.243), custom_call_target="tpu_custom_call" | custom-call | tf_op jit(solution)/shard_map/pallas_call | solution.py:255
  380.1 12.4 %shard_map.287 = bf16[2,1024,384]{2,1,0:T(8,128)(2,1)S(1)} custom-call(bf16[2,1024,384]{2,1,0:T(8,128)(2,1)S(1)} %copy-done.4, s32[2,1024,1]{2,1,0:T(8,128)S(1)} %copy.94.first_ref, f32[2,1024,128]{2,1,0:T(8,128)S(1)} %copy-done.13, bf16[2,1024,128]{2,1,0:T(8,128)(2,1)S(1)} %shard_map.286.back_ref), custom_call_target="tpu_custom_call" | custom-call | tf_op jit(solution)/shard_map/pallas_call | solution.py:360
  397.6 34.4 %all-reduce.6.cloned.1.call-done = bf16[8,4,32,1031]{3,2,0,1:T(8,128)(2,1)} async-done(((bf16[8,4,32,1031]{3,2,0,1:T(8,128)(2,1)}), bf16[8,4,32,1031]{3,2,0,1:T(8,128)(2,1)}) %all-reduce.6.cloned.1.call-update) | async-done | bytes 2111504
  434.4 6.2 convolution_convert_fusion.9
  440.6 6.2 convolution_convert_fusion.8
  447.0 8.8 %convolution_convert_fusion.4 = bf16[4,512,1024]{2,1,0:T(8,128)(2,1)} fusion(bf16[4,640,512]{2,1,0:T(8,128)(2,1)} %get-tuple-element.125, bf16[4,640,1024]{2,1,0:T(8,128)(2,1)} %bitcast.260), kind=kOutput, calls=%fused_computation.39 | convolution fusion | flops 2686451712 | bytes 12058624 | tf_op jit(solution)/shard_map/etk,etf->ekf/dot_general | solution.py:482
  455.9 8.7 %convolution_convert_fusion.5 = bf16[4,1024,512]{2,1,0:T(8,128)(2,1)} fusion(bf16[4,640,1024]{2,1,0:T(8,128)(2,1)} %bitcast.258, bf16[4,640,512]{2,1,0:T(8,128)(2,1)} %fusion.11), kind=kOutput, calls=%fused_computation.40 | convolution fusion | flops 2686451712 | bytes 12058624 | tf_op jit(solution)/shard_map/etf,etk->efk/dot_general | solution.py:482
  469.6 49.1 %shard_map.288 = f32[2,128,1024]{2,1,0:T(8,128)S(1)} custom-call(bf16[2,8,128,1024]{3,2,1,0:T(8,128)(2,1)S(1)} %bitcast.238), custom_call_target="tpu_custom_call" | custom-call | tf_op jit(solution)/shard_map/pallas_call | solution.py:197
  541.9 7.7 %reduce-scatter.24.cloned.1.call-done = bf16[128,1024]{1,0:T(8,128)(2,1)} async-done(((bf16[512,1024]{1,0:T(8,128)(2,1)}), bf16[128,1024]{1,0:T(8,128)(2,1)}) %reduce-scatter.24.cloned.1.call-update) | async-done | bytes 262160 | tf_op jit(solution)/shard_map/reduce_scatter | solution.py:534
  554.9 50.5 %reduce-scatter.32.cloned.1.call-done = bf16[1,512,1024]{2,1,0:T(8,128)(2,1)} async-done(((bf16[4,512,1024]{2,1,0:T(8,128)(2,1)}), bf16[1,512,1024]{2,1,0:T(8,128)(2,1)}) %reduce-scatter.32.cloned.1.call-update) | async-done | bytes 1048592
  608.2 52.9 %reduce-scatter.30.cloned.1.call-done = bf16[1,1024,512]{2,1,0:T(8,128)(2,1)} async-done(((bf16[4,1024,512]{2,1,0:T(8,128)(2,1)}), bf16[1,1024,512]{2,1,0:T(8,128)(2,1)}) %reduce-scatter.30.cloned.1.call-update) | async-done | bytes 1048592
  664.0 49.5 %reduce-scatter.18.cloned.1.call-done = bf16[2,128,1024]{2,1,0:T(8,128)(2,1)} async-done(((bf16[2,1024,1024]{2,1,0:T(8,128)(2,1)}), bf16[2,128,1024]{2,1,0:T(8,128)(2,1)}) %reduce-scatter.18.cloned.1.call-update) | async-done | bytes 524304 | tf_op jit(solution)/shard_map/reduce_scatter | solution.py:502
  (220 shorter events, 148.2 us)
Async XLA Ops:
  7.2 97.2 %copy-start = (bf16[1024,1024]{1,0:T(8,128)(2,1)S(1)}, bf16[1024,1024]{1,0:T(8,128)(2,1)}, u32[]{:S(2)}) copy-start(bf16[1024,1024]{1,0:T(8,128)(2,1)} %param.28) | copy-start | bytes 6291460
  7.2 204.9 %all-gather.6.cloned.1.call-start = ((), (), s32[]{:S(2)}) async-start(), calls=%async_computation.10 | async-start | bytes 5242880 | tf_op jit(solution)/shard_map/all_gather | solution.py:423
  7.9 213.0 %all-gather.8.cloned.1.call-start = ((), (), s32[]{:S(2)}) async-start(), calls=%async_computation.11 | async-start | bytes 5242880 | tf_op jit(solution)/shard_map/all_gather | solution.py:424
  8.7 221.3 %all-gather.10.cloned.1.call-start = ((), (), s32[]{:S(2)}) async-start(), calls=%async_computation.16 | async-start | bytes 4718592 | tf_op jit(solution)/shard_map/all_gather | solution.py:422
  9.4 330.3 %reduce-scatter.26.cloned.1.call-start = ((), (), s32[]{:S(2)}) async-start(), calls=%async_computation.17 | async-start | bytes 589824
  33.8 42.3 %copy-start.24 = (bf16[1024,128]{1,0:T(8,128)(2,1)}, bf16[1024,128]{1,0:T(8,128)(2,1)S(1)}, u32[]{:S(2)}) copy-start(bf16[1024,128]{1,0:T(8,128)(2,1)S(1)} %constant_dynamic-slice_fusion.8) | copy-start | bytes 786436
  35.3 38.4 %copy-start.26 = (bf16[1024,128]{1,0:T(8,128)(2,1)S(1)}, bf16[1024,128]{1,0:T(8,128)(2,1)}, u32[]{:S(2)}) copy-start(bf16[1024,128]{1,0:T(8,128)(2,1)} %get-tuple-element.133) | copy-start | bytes 786436
  35.3 38.4 %copy-start.28 = (bf16[1024,128]{1,0:T(8,128)(2,1)S(1)}, bf16[1024,128]{1,0:T(8,128)(2,1)}, u32[]{:S(2)}) copy-start(bf16[1024,128]{1,0:T(8,128)(2,1)} %get-tuple-element.134) | copy-start | bytes 786436
  106.4 72.7 %copy-start.31 = (bf16[1024,2]{0,1:T(2,128)(2,1)S(1)}, bf16[1024,2]{0,1:T(2,128)(2,1)}, u32[]{:S(2)}) copy-start(bf16[1024,2]{0,1:T(2,128)(2,1)} %param.33) | copy-start | bytes 12292
  107.4 73.0 %copy-start.5 = (bf16[256,1024]{1,0:T(8,128)(2,1)}, bf16[256,1024]{1,0:T(8,128)(2,1)S(1)}, u32[]{:S(2)}) copy-start(bf16[256,1024]{1,0:T(8,128)(2,1)S(1)} %multiply_convert_fusion.6) | copy-start | bytes 1572868
  107.4 73.1 %copy-start.30 = (bf16[1024,4]{0,1:T(4,128)(2,1)S(1)}, bf16[1024,4]{0,1:T(4,128)(2,1)}, u32[]{:S(2)}) copy-start(bf16[1024,4]{0,1:T(4,128)(2,1)} %param.32) | copy-start | bytes 24580
  254.9 177.0 %all-reduce.6.cloned.1.call-start = ((), (), s32[]{:S(2)}) async-start(), calls=%async_computation.18 | async-start | bytes 4718592
  357.3 163.1 %reduce-scatter.20.cloned.1.call-start = ((), (), s32[]{:S(2)}) async-start(), calls=%async_computation.13 | async-start | bytes 983040 | tf_op jit(solution)/shard_map/reduce_scatter | solution.py:537
  396.9 126.9 %reduce-scatter.28.cloned.1.call-start = ((), (), s32[]{:S(2)}) async-start(), calls=%async_computation.19 | async-start | bytes 368640
  434.3 100.2 %reduce-scatter.22.cloned.1.call-start = ((), (), s32[]{:S(2)}) async-start(), calls=%async_computation.14 | async-start | bytes 1310720 | tf_op jit(solution)/shard_map/reduce_scatter | solution.py:537
  440.6 109.0 %reduce-scatter.24.cloned.1.call-start = ((), (), s32[]{:S(2)}) async-start(), calls=%async_computation.15 | async-start | bytes 1310720 | tf_op jit(solution)/shard_map/reduce_scatter | solution.py:534
  446.8 158.6 %reduce-scatter.32.cloned.1.call-start = ((), (), s32[]{:S(2)}) async-start(), calls=%async_computation.21 | async-start | bytes 5242880
  455.9 205.3 %reduce-scatter.30.cloned.1.call-start = ((), (), s32[]{:S(2)}) async-start(), calls=%async_computation.20 | async-start | bytes 5242880
  464.7 248.8 %reduce-scatter.18.cloned.1.call-start = ((), (), s32[]{:S(2)}) async-start(), calls=%async_computation.12 | async-start | bytes 4718592 | tf_op jit(solution)/shard_map/reduce_scatter | solution.py:502
  469.5 49.1 %copy-start.17 = (bf16[1,2,128,1024]{3,2,1,0:T(8,128)(2,1)S(1)}, bf16[1,2,128,1024]{3,2,1,0:T(8,128)(2,1)}, u32[]{:S(2)}) copy-start(bf16[1,2,128,1024]{3,2,1,0:T(8,128)(2,1)} %param.18) | copy-start | bytes 1572868
  469.5 49.5 %copy-start.19 = (f32[256,1024]{1,0:T(8,128)S(1)}, f32[256,1024]{1,0:T(8,128)}, u32[]{:S(2)}) copy-start(f32[256,1024]{1,0:T(8,128)} %copy-done.18) | copy-start | bytes 3145732
  520.4 11.7 %all-to-all-start = ((bf16[8,32,384]{2,1,0:T(8,128)(2,1)}), bf16[8,32,384]{2,1,0:T(8,128)(2,1)S(1)}, u32[]{:S(2)}, u32[]{:S(2)}) async-start(bf16[8,32,384]{2,1,0:T(8,128)(2,1)} %bitcast.279), calls=%async_computation.2 | async-start | bytes 393216 | tf_op jit(solution)/shard_map/all_to_all | solution.py:538
  534.5 16.9 %all-to-all-start.1 = ((bf16[8,32,512]{2,1,0:T(8,128)(2,1)}), bf16[8,32,512]{2,1,0:T(8,128)(2,1)S(1)}, u32[]{:S(2)}, u32[]{:S(2)}) async-start(bf16[8,32,512]{2,1,0:T(8,128)(2,1)} %bitcast.278), calls=%async_computation.4 | async-start | bytes 524288 | tf_op jit(solution)/shard_map/all_to_all | solution.py:538
  552.4 161.1 %copy-start.16 = (f32[256,1024]{1,0:T(8,128)S(1)}, f32[256,1024]{1,0:T(8,128)}, u32[]{:S(2)}) copy-start(f32[256,1024]{1,0:T(8,128)} %copy-done.15) | copy-start | bytes 3145732
  (28 other events, 179.4 us)
Sparse Core Ops, SparseCore 0:
  9.9 55.3 all-gather.5
  67.2 52.6 all-gather.7
  121.5 58.3 all-gather.9
  255.0 29.2 reduce-scatter.25
  357.4 74.5 all-reduce.5
  434.9 25.2 reduce-scatter.19
  463.8 24.1 reduce-scatter.27
  491.2 27.7 reduce-scatter.21
  521.9 27.7 reduce-scatter.23
  552.7 52.6 reduce-scatter.31
  608.4 52.6 reduce-scatter.29
  663.4 49.9 reduce-scatter.17

commit v2 on v1

--- a/solution.py
+++ b/solution.py
@@ -144,72 +144,57 @@
     )(x)
 
 
-def scatter_kernel(x_ref, out_ref, pair_buf, comb, far_buf, send_sem, recv_sem, pair_send, pair_recv):
-    micro_count, cut_count, rows, width = x_ref.shape
+def scatter_kernel(
+    x_ref, dots_ref, out_ref, sums_ref, pair_buf, comb, far_buf, dots_in, pair_send, pair_recv, send, recv, dot_send, dot_recv
+):
+    micro_count, cut_count = x_ref.shape[:2]
     cut = lax.axis_index("cuts")
-    group = lax.axis_index("expert")
-    sibling = jnp.bitwise_xor(cut, 1)
-    side = cut % 2
-    levels = cut_count // 2
-    greet_line(cut_count, False)
-    hops = [levels - 1 - k for k in range(levels)]
-
-    def pair_copy(m, k):
-        dest = jnp.bitwise_xor(cut, 2 * k)
-        return pltpu.make_async_remote_copy(
-            src_ref=x_ref.at[m, jnp.bitwise_xor(dest, 1)], dst_ref=pair_buf.at[m, k],
-            send_sem=pair_send.at[m, k], recv_sem=pair_recv.at[m, k],
-            device_id=(group, sibling), device_id_type=MESH)
-
-    def far_copy(m, k):
-        return pltpu.make_async_remote_copy(
-            src_ref=comb.at[m, k], dst_ref=far_buf.at[m, k],
-            send_sem=send_sem.at[m, k], recv_sem=recv_sem.at[m, k],
-            device_id=(group, jnp.bitwise_xor(cut, 2 * k)), device_id_type=MESH)
+    greet_line(cut_count, True)
+    line = LineSum(x_ref, pair_buf, comb, far_buf, pair_send, pair_recv, send, recv)
+
+    def dot_copy(hop):
+        target = jnp.bitwise_xor(cut, hop)
+        return line_copy(
+            dots_ref.at[target], dots_in.at[hop - 1], dot_send.at[hop - 1], dot_recv.at[hop - 1], line.group, target
+        )
 
     for m in range(micro_count):
-        for k in hops:
-            pair_copy(m, k).start()
+        line.start(m)
+    for hop in range(1, cut_count):
+        dot_copy(hop).start()
     for m in range(micro_count):
-        for k in hops:
-            pair_copy(m, k).wait_recv()
-            total = x_ref[m, jnp.bitwise_xor(cut, 2 * k)].astype(jnp.float32) + pair_buf[m, k].astype(jnp.float32)
-            if k:
-                comb[m, k] = total.astype(comb.dtype)
-                far_copy(m, k).start()
-            else:
-                out_ref[m] = total
+        line.forward(m)
+    sums = dots_ref[cut]
+    for hop in range(1, cut_count):
+        dot_copy(hop).wait()
+        sums = sums + dots_in[hop - 1]
+    sums_ref[...] = sums
     for m in range(micro_count):
-        for k in hops:
-            if k:
-                far_copy(m, k).wait_recv()
-                out_ref[m] = out_ref[m] + far_buf[m, k].astype(jnp.float32)
-    for m in range(micro_count):
-        for k in hops:
-            pair_copy(m, k).wait_send()
-            if k:
-                far_copy(m, k).wait_send()
-
-
-def cut_scatter(x, call_id):
+        out_ref[m] = line.finish(m)
+
+
+def cut_scatter(x, dots, call_id):
     micro_count, cut_count, rows, width = x.shape
     levels = cut_count // 2
+    dma = pltpu.SemaphoreType.DMA
     return pl.pallas_call(
         scatter_kernel,
-        out_shape=jax.ShapeDtypeStruct((micro_count, rows, width), jnp.float32),
-        in_specs=[pl.BlockSpec(memory_space=pltpu.VMEM)],
-        out_specs=pl.BlockSpec(memory_space=pltpu.VMEM),
+        out_shape=(
+            jax.ShapeDtypeStruct((micro_count, rows, width), jnp.float32),
+            jax.ShapeDtypeStruct(dots.shape[1:], jnp.float32),
+        ),
+        in_specs=[pl.BlockSpec(memory_space=pltpu.VMEM)] * 2,
+        out_specs=[pl.BlockSpec(memory_space=pltpu.VMEM)] * 2,
         scratch_shapes=[
             pltpu.VMEM((micro_count, levels, rows, width), x.dtype),
             pltpu.VMEM((micro_count, levels, rows, width), x.dtype),
             pltpu.VMEM((micro_count, levels, rows, width), x.dtype),
-            pltpu.SemaphoreType.DMA((micro_count, levels)),
-            pltpu.SemaphoreType.DMA((micro_count, levels)),
-            pltpu.SemaphoreType.DMA((micro_count, levels)),
-            pltpu.SemaphoreType.DMA((micro_count, levels)),
+            pltpu.VMEM((cut_count - 1, *dots.shape[1:]), jnp.float32),
+            dma((micro_count, levels)), dma((micro_count, levels)), dma((micro_count, levels)), dma((micro_count, levels)),
+            dma((cut_count - 1,)), dma((cut_count - 1,)),
         ],
         compiler_params=pltpu.CompilerParams(collective_id=call_id, has_side_effects=True, vmem_limit_bytes=48 * 2**20),
-    )(x)
+    )(x, dots)
 
 
 def swap_kernel(to_rows, x_ref, out_ref, send_sem, recv_sem, own_sem):
@@ -272,10 +257,10 @@
     return [((lane >= h * size) & (lane < (h + 1) * size)) for h in range(heads)]
 
 
-def allowed_mask(first_ref, start, rows, keys):
+def allowed_mask(first_ref, m, start, rows, keys):
     query_spots = start + lax.broadcasted_iota(jnp.int32, (rows, keys), 0)
     key_spots = lax.broadcasted_iota(jnp.int32, (rows, keys), 1)
-    return (key_spots <= query_spots) & (key_spots >= first_ref[0, pl.ds(start, rows), :])
+    return (key_spots <= query_spots) & (key_spots >= first_ref[m, pl.ds(start, rows), :])
 
 
 def attend_kernel(heads, qkv_ref, first_ref, att_ref, lse_ref):
@@ -284,7 +269,7 @@
     masks = head_masks(width, heads)
     for block in range(length // rows):
         start, keys = block * rows, (block + 1) * rows
-        allowed = allowed_mask(first_ref, start, rows, keys)
+        allowed = allowed_mask(first_ref, 0, start, rows, keys)
         query = qkv_ref[0, pl.ds(start, rows), 0:width] * jnp.bfloat16(score_scale)
         key = qkv_ref[0, 0:keys, width : 2 * width]
         value = qkv_ref[0, 0:keys, 2 * width : 3 * width]
@@ -320,7 +305,233 @@
     )(qkv, first)
 
 
-def attend_back_kernel(heads, qkv_ref, first_ref, lse_ref, back_ref, out_ref, key_acc, value_acc):
+def norm_parts(values):
+    center = values - jnp.mean(values, axis=-1, keepdims=True)
+    spread = jnp.mean(center * center, axis=-1, keepdims=True)
+    scale = lax.rsqrt(spread + norm_eps)
+    return center * scale, scale
+
+
+def norm_back(normed, scale, gain, grad):
+    inner = grad * gain
+    return scale * (
+        inner
+        - jnp.mean(inner, axis=-1, keepdims=True)
+        - normed * jnp.mean(inner * normed, axis=-1, keepdims=True)
+    )
+
+
+def gelu_pair(values):
+    phi = 0.5 * (1.0 + lax.erf(values * (0.5**0.5)))
+    bell = jnp.exp(-0.5 * values * values) * ((2.0 * jnp.pi) ** -0.5)
+    return values * phi, phi + values * bell
+
+
+def tile_slots(capacity, row_count, tile):
+    return -(-capacity * (tile // row_count) // 16) * 16
+
+
+def token_table(spot, width):
+    return (spot == lax.broadcasted_iota(jnp.int32, (spot.shape[0], width), 1)).astype(jnp.bfloat16)
+
+
+def lane_softmax(logits, lanes, first, count):
+    inside = (lanes >= first) & (lanes < first + count)
+    raised = jnp.exp(logits - jnp.max(jnp.where(inside, logits, masked_value), axis=-1, keepdims=True))
+    raised = jnp.where(inside, raised, 0.0)
+    return raised / jnp.sum(raised, axis=-1, keepdims=True)
+
+
+def route(logits, chosen, expert_count):
+    lanes = lax.broadcasted_iota(jnp.int32, logits.shape, 1)
+    routed = lane_softmax(logits, lanes, 0, expert_count)
+    mixing = lane_softmax(logits, lanes, expert_count, 2)
+    pick = lambda values, lane: jnp.sum(jnp.where(lanes == lane, values, 0.0), axis=-1, keepdims=True)
+    return pick(routed, chosen), pick(mixing, expert_count), pick(mixing, expert_count + 1), routed, mixing
+
+
+def feed_kernel(
+    tile, slots, h_ref, g_ref, chosen_ref, spot_ref, small_ref, own_in_ref, own_out_ref, in_ref, out_w_ref,
+    out_ref, back_ref, dots_ref, d_own_in_ref, d_own_out_ref, d_in_ref, d_out_ref,
+    sent, g_sent, hidden_buf, pre_buf, gate_buf, dots_buf,
+):
+    step = pl.program_id(0)
+    expert_count = sent.shape[0]
+    total, features = h_ref.shape
+    tiles = total // tile
+    low = jnp.bfloat16
+    lanes = lax.broadcasted_iota(jnp.int32, (tile, 128), 1)
+
+    @pl.when(step == 0)
+    def _():
+        def one(t, carry):
+            rows = pl.ds(pl.multiple_of(t * tile, tile), tile)
+            spots = pl.ds(pl.multiple_of(t * slots, slots), slots)
+            h_two = h_ref[rows, :]
+            gate, mix_dense, mix_expert, _, _ = route(plain_dot(h_two, small_ref[...]), chosen_ref[rows, :], expert_count)
+            mix_gate = mix_expert * gate
+            gate_buf[rows, :] = jnp.broadcast_to(mix_gate, (tile, 128))
+            table = token_table(spot_ref[rows, :], expert_count * slots)
+            grad_y = g_ref[rows, :].astype(jnp.float32)
+            rows_sent = lead_dot(table, h_two).astype(low)
+            rows_back = lead_dot(table, (mix_gate * grad_y).astype(low)).astype(low)
+            for e in range(expert_count):
+                sent[e, spots, :] = rows_sent[e * slots : (e + 1) * slots]
+                g_sent[e, spots, :] = rows_back[e * slots : (e + 1) * slots]
+            act, slope = gelu_pair(plain_dot(h_two, own_in_ref[...]))
+            dense = plain_dot(act.astype(low), own_out_ref[...])
+            dots_buf[rows, :] = jnp.where(lanes == 0, jnp.sum(grad_y * dense, axis=-1, keepdims=True), 0.0)
+            d_pre = (tail_dot((mix_dense * grad_y).astype(low), own_out_ref[...]) * slope).astype(low)
+            hidden_buf[rows, :] = (mix_dense * act).astype(low)
+            pre_buf[rows, :] = d_pre
+            out_ref[rows, :] = (mix_dense * dense).astype(low)
+            back_ref[rows, :] = tail_dot(d_pre, own_in_ref[...]).astype(low)
+            return carry
+
+        lax.fori_loop(0, tiles, one, 0)
+
+    @pl.when((step >= 1) & (step <= expert_count))
+    def _():
+        e = step - 1
+        rows_in, rows_back = sent[e], g_sent[e]
+        act, slope = gelu_pair(plain_dot(rows_in, in_ref[0]))
+        inner = act.astype(low)
+        d_pre = (tail_dot(rows_back, out_w_ref[0]) * slope).astype(low)
+        d_in_ref[0] = lead_dot(rows_in, d_pre).astype(low)
+        d_out_ref[0] = lead_dot(inner, rows_back).astype(low)
+        sent[e] = tail_dot(d_pre, in_ref[0]).astype(low)
+        g_sent[e] = plain_dot(inner, out_w_ref[0]).astype(low)
+
+    @pl.when(step == expert_count + 1)
+    def _():
+        def one(t, carry):
+            rows = pl.ds(pl.multiple_of(t * tile, tile), tile)
+            spots = pl.ds(pl.multiple_of(t * slots, slots), slots)
+            table = token_table(spot_ref[rows, :], expert_count * slots)
+            grad_y = g_ref[rows, :].astype(jnp.float32)
+            gather = lambda ref: jnp.concatenate([ref[e, spots, :] for e in range(expert_count)], axis=0)
+            part = plain_dot(table, gather(g_sent))
+            dots = jnp.where(lanes == 1, jnp.sum(grad_y * part, axis=-1, keepdims=True), dots_buf[rows, :])
+            for k in range(tile // 128):
+                dots_ref[t * (tile // 128) + k] = jnp.transpose(dots[k * 128 : (k + 1) * 128])[0:8]
+            out_ref[rows, :] = (out_ref[rows, :].astype(jnp.float32) + gate_buf[rows, 0:1] * part).astype(low)
+            back = plain_dot(table, gather(sent))
+            back_ref[rows, :] = (back_ref[rows, :].astype(jnp.float32) + back).astype(low)
+            return carry
+
+        lax.fori_loop(0, tiles, one, 0)
+        width = 256
+        for k in range(features // width):
+            part = slice(k * width, (k + 1) * width)
+            d_own_in_ref[part, :] = lead_dot(h_ref[:, part], pre_buf[...]).astype(low)
+            d_own_out_ref[:, part] = lead_dot(hidden_buf[...], g_ref[:, part]).astype(low)
+
+
+def feed(h_all, g_all, chosen, spot, small, own_in, own_out, weights_in, weights_out, tile, slots):
+    total, features = h_all.shape
+    expert_count, _, share = weights_in.shape
+    low, f32 = jnp.bfloat16, jnp.float32
+    whole = lambda x: pl.BlockSpec(x.shape, lambda i: (0,) * len(x.shape), pipeline_mode=pl.Buffered(1))
+    expert = lambda r, c: pl.BlockSpec((1, r, c), lambda i: (jnp.clip(i - 1, 0, expert_count - 1), 0, 0))
+    outs = (
+        jax.ShapeDtypeStruct((total, features), low),
+        jax.ShapeDtypeStruct((total, features), low),
+        jax.ShapeDtypeStruct((total // 128, 8, 128), f32),
+        jax.ShapeDtypeStruct((features, share), low),
+        jax.ShapeDtypeStruct((share, features), low),
+        jax.ShapeDtypeStruct((expert_count, features, share), low),
+        jax.ShapeDtypeStruct((expert_count, share, features), low),
+    )
+    rows = total // tile * slots
+    return pl.pallas_call(
+        partial(feed_kernel, tile, slots),
+        grid=(expert_count + 2,),
+        out_shape=outs,
+        in_specs=[whole(x) for x in (h_all, g_all, chosen, spot, small, own_in, own_out)]
+        + [expert(features, share), expert(share, features)],
+        out_specs=[whole(x) for x in outs[:5]] + [expert(features, share), expert(share, features)],
+        scratch_shapes=[
+            pltpu.VMEM((expert_count, rows, features), low),
+            pltpu.VMEM((expert_count, rows, features), low),
+            pltpu.VMEM((total, share), low),
+            pltpu.VMEM((total, share), low),
+            pltpu.VMEM((total, 128), f32),
+            pltpu.VMEM((total, 128), f32),
+        ],
+        compiler_params=pltpu.CompilerParams(vmem_limit_bytes=60 * 2**20),
+    )(h_all, g_all, chosen, spot, small, own_in, own_out, weights_in, weights_out)
+
+
+def softmax_back(probs, grad):
+    return probs * (grad - jnp.sum(probs * grad, axis=-1, keepdims=True))
+
+
+def line_copy(src, dst, send, recv, group, target):
+    return pltpu.make_async_remote_copy(
+        src_ref=src, dst_ref=dst, send_sem=send, recv_sem=recv, device_id=(group, target), device_id_type=MESH
+    )
+
+
+def greet_all(cut_count, group_count):
+    cut = lax.axis_index("cuts")
+    group = lax.axis_index("expert")
+    barrier = pltpu.get_barrier_semaphore()
+    for hop in range(1, cut_count):
+        pl.semaphore_signal(barrier, inc=1, device_id=(group, jnp.bitwise_xor(cut, hop)), device_id_type=MESH)
+    for hop in range(1, group_count):
+        pl.semaphore_signal(barrier, inc=1, device_id=(lax.rem(group + hop, group_count), cut), device_id_type=MESH)
+    pl.semaphore_wait(barrier, cut_count + group_count - 2)
+
+
+class LineSum:
+    def __init__(self, part, pair_buf, comb, far_buf, pair_send, pair_recv, send, recv):
+        self.refs = (part, pair_buf, comb, far_buf, pair_send, pair_recv, send, recv)
+        self.cut = lax.axis_index("cuts")
+        self.group = lax.axis_index("expert")
+        self.levels = part.shape[1] // 2
+        self.order = list(range(self.levels - 1, -1, -1))
+
+    def pair_copy(self, m, k):
+        part, pair_buf, _, _, pair_send, pair_recv, _, _ = self.refs
+        return line_copy(
+            part.at[m, jnp.bitwise_xor(self.cut, 2 * k + 1)], pair_buf.at[m, k], pair_send.at[m, k], pair_recv.at[m, k],
+            self.group, jnp.bitwise_xor(self.cut, 1),
+        )
+
+    def far_copy(self, m, k):
+        _, _, comb, far_buf, _, _, send, recv = self.refs
+        return line_copy(
+            comb.at[m, k], far_buf.at[m, k], send.at[m, k], recv.at[m, k], self.group, jnp.bitwise_xor(self.cut, 2 * k)
+        )
+
+    def start(self, m):
+        for k in self.order:
+            self.pair_copy(m, k).start()
+
+    def forward(self, m):
+        part, pair_buf, comb = self.refs[:3]
+        for k in self.order:
+            self.pair_copy(m, k).wait_recv()
+            total = part[m, jnp.bitwise_xor(self.cut, 2 * k)].astype(jnp.float32) + pair_buf[m, k].astype(jnp.float32)
+            comb[m, k] = total.astype(comb.dtype)
+            if k:
+                self.far_copy(m, k).start()
+
+    def finish(self, m):
+        comb, far_buf = self.refs[2:4]
+        total = comb[m, 0].astype(jnp.float32)
+        for k in self.order:
+            if k:
+                self.far_copy(m, k).wait_recv()
+                total = total + far_buf[m, k].astype(jnp.float32)
+        for k in self.order:
+            self.pair_copy(m, k).wait_send()
+            if k:
+                self.far_copy(m, k).wait_send()
+        return total
+
+
+def attend_back_one(heads, m, qkv_ref, first_ref, lse_ref, back_ref, out_ref, key_acc, value_acc):
     length, width = back_ref.shape[1], back_ref.shape[2]
     rows = min(256, length)
     masks = head_masks(width, heads)
@@ -329,12 +540,12 @@
     zero = jnp.bfloat16(0)
     for block in range(length // rows):
         start, keys = block * rows, (block + 1) * rows
-        allowed = allowed_mask(first_ref, start, rows, keys)
-        query = qkv_ref[0, pl.ds(start, rows), 0:width] * jnp.bfloat16(score_scale)
-        key = qkv_ref[0, 0:keys, width : 2 * width]
-        value = qkv_ref[0, 0:keys, 2 * width : 3 * width]
-        back = back_ref[0, pl.ds(start, rows), :]
-        logs = lse_ref[0, pl.ds(start, rows), :]
+        allowed = allowed_mask(first_ref, m, start, rows, keys)
+        query = qkv_ref[m, pl.ds(start, rows), 0:width] * jnp.bfloat16(score_scale)
+        key = qkv_ref[m, 0:keys, width : 2 * width]
+        value = qkv_ref[m, 0:keys, 2 * width : 3 * width]
+        back = back_ref[m, pl.ds(start, rows), :]
+        logs = lse_ref[m, pl.ds(start, rows), :]
         query_grad = jnp.zeros((rows, width), jnp.float32)
         for h, mask in enumerate(masks):
             one_query = jnp.where(mask, query, zero)
@@ -342,56 +553,278 @@
             scores = jnp.where(allowed, tail_dot(one_query, key), masked_value)
             spot = h * (width // heads)
             probs = jnp.exp(scores - logs[:, spot : spot + 1])
-            dprobs = tail_dot(one_back, value)
-            weighted = probs * dprobs
+            weighted = probs * tail_dot(one_back, value)
             delta = jnp.sum(weighted, axis=-1, keepdims=True)
             score_grad = (weighted - probs * delta).astype(jnp.bfloat16)
             query_grad = jnp.where(mask, plain_dot(score_grad, key), query_grad)
             key_acc[0:keys, :] += lead_dot(score_grad, one_query)
             value_acc[0:keys, :] += lead_dot(probs.astype(jnp.bfloat16), one_back)
-        out_ref[0, pl.ds(start, rows), 0:width] = (query_grad * score_scale).astype(jnp.bfloat16)
-    out_ref[0, :, width : 2 * width] = key_acc[...].astype(jnp.bfloat16)
-    out_ref[0, :, 2 * width : 3 * width] = value_acc[...].astype(jnp.bfloat16)
-
-
-def attend_back(qkv, first, lse, back, heads):
-    micro_count, length, width = back.shape
-    block = lambda w: pl.BlockSpec((1, length, w), lambda m: (m, 0, 0))
+        out_ref[m, pl.ds(start, rows), 0:width] = (query_grad * score_scale).astype(jnp.bfloat16)
+    out_ref[m, :, width : 2 * width] = key_acc[...].astype(jnp.bfloat16)
+    out_ref[m, :, 2 * width : 3 * width] = value_acc[...].astype(jnp.bfloat16)
+
+
+def back_kernel(
+    heads, expert_count, sums_here,
+    dh_ref, dots_ref, chosen_ref, h_ref, x_two_ref, gy_ref, att_ref, w_out_ref, qkv_ref, first_ref, lse_ref, w_qkv_ref,
+    h_all_ref, x_ref, gain_one_ref, gain_two_ref, small_ref, own_in_ref, own_out_ref, w_rows_ref,
+    tokens_ref, wo_ref, small_out_ref, qkv_out_ref, in_out_ref, out_out_ref, norm_ref,
+    d_x_two, g_att, d_att, back_all, d_qkv, key_acc, value_acc, d_small, part, pair_buf, comb, far_buf,
+    wo_part, qkv_part, wo_in, qkv_in, own_in_in, own_out_in, wo_mid, qkv_mid, in_mid, wo_end, qkv_end, in_end,
+    pair_send, pair_recv, far_send, far_recv, swap_send, swap_recv, swap_own, one_send, one_recv, two_send, two_recv, two_own,
+):
+    micro_count, cut_count, rows, features = part.shape
+    group_count, split, piece_rows, _ = wo_part.shape
+    group_rows = split * piece_rows
+    width = features // cut_count
+    cut = lax.axis_index("cuts")
+    group = lax.axis_index("expert")
+    low, f32 = jnp.bfloat16, jnp.float32
+    greet_all(cut_count, group_count if sums_here else 1)
+
+    ones = ((own_in_ref, own_in_in), (own_out_ref, own_out_in), (wo_part, wo_in), (qkv_part, qkv_in))
+
+    def one_copy(kind, hop):
+        src, dst = ones[kind]
+        target = lax.rem(group + hop, group_count)
+        return line_copy(
+            src.at[target], dst.at[hop - 1], one_send.at[kind, hop - 1], one_recv.at[kind, hop - 1], target, cut
+        )
+
+    def one_start(kind):
+        for hop in range(1, group_count):
+            one_copy(kind, hop).start()
+
+    def one_finish(kind):
+        src, dst = ones[kind]
+        total = src[group].astype(f32)
+        for hop in range(1, group_count):
+            one_copy(kind, hop).wait_recv()
+            total = total + dst[hop - 1].astype(f32)
+        for hop in range(1, group_count):
+            one_copy(kind, hop).wait_send()
+        return total
+
+    twos = ((in_mid, in_end), None, (wo_mid, wo_end), (qkv_mid, qkv_end))
+
+    def two_copy(kind, hop):
+        src, dst = twos[kind]
+        target = jnp.bitwise_xor(cut, hop)
+        return line_copy(src.at[target], dst.at[cut], two_send.at[kind, hop], two_recv.at[kind, hop], group, target)
+
+    def two_keep(kind):
+        src, dst = twos[kind]
+        return pltpu.make_async_copy(src.at[cut], dst.at[cut], two_own.at[kind])
+
+    def two_start(kind):
+        for hop in range(cut_count - 1, 0, -1):
+            two_copy(kind, hop).start()
+        two_keep(kind).start()
+
+    def two_finish(kind):
+        for hop in range(cut_count - 1, 0, -1):
+            two_copy(kind, hop).wait()
+        two_keep(kind).wait()
+
+    if sums_here:
+        one_start(0)
+        one_start(1)
+
+    def swap_copy(m, hop):
+        target = jnp.bitwise_xor(cut, hop)
+        return line_copy(
+            d_att.at[m, :, pl.ds(pl.multiple_of(target * width, width), width)],
+            back_all.at[m, pl.ds(pl.multiple_of(cut * rows, rows), rows), :],
+            swap_send.at[m, hop], swap_recv.at[m, hop], group, target,
+        )
+
+    def swap_keep(m):
+        return pltpu.make_async_copy(
+            d_att.at[m, :, pl.ds(pl.multiple_of(cut * width, width), width)],
+            back_all.at[m, pl.ds(pl.multiple_of(cut * rows, rows), rows), :],
+            swap_own.at[m],
+        )
+
+    small = small_ref[...]
+    gain_two = gain_two_ref[...]
+    d_small[...] = jnp.zeros_like(d_small)
+    lanes = lax.broadcasted_iota(jnp.int32, (rows, 128), 1)
+
+    def norm_two_step(m, carry):
+        dots = jnp.transpose(dots_ref[m])
+        chosen = chosen_ref[m]
+        h_two = h_ref[m]
+        gate, _, mix_expert, routed, mixing = route(plain_dot(h_two, small), chosen, expert_count)
+        d_mixing = jnp.where(lanes == expert_count, dots[:, 0:1], gate * dots[:, 1:2])
+        d_gate = jnp.where(lanes == chosen, mix_expert * dots[:, 1:2], 0.0)
+        d_logits = (softmax_back(mixing, d_mixing) + softmax_back(routed, d_gate)).astype(low)
+        d_h = dh_ref[m] + tail_dot(d_logits, small)
+        normed, scale = norm_parts(x_two_ref[m])
+        one_lane = (lanes == expert_count + 2).astype(low)
+        d_small[...] += lead_dot(h_two, d_logits) + lead_dot((d_h * normed).astype(low), one_lane)
+        d_x = gy_ref[m].astype(f32) + norm_back(normed, scale, gain_two, d_h)
+        d_x_two[m] = d_x
+        grad = d_x.astype(low)
+        g_att[pl.ds(pl.multiple_of(m * rows, rows), rows), :] = grad
+        d_att[m] = tail_dot(grad, w_out_ref[...]).astype(low)
+        for hop in range(cut_count - 1, 0, -1):
+            swap_copy(m, hop).start()
+        swap_keep(m).start()
+        return carry
+
+    lax.fori_loop(0, micro_count, norm_two_step, 0)
+
+    def wo_step(g, carry):
+        columns = pl.ds(pl.multiple_of(g * group_rows, group_rows), group_rows)
+        grads = lead_dot(att_ref[:, columns], g_att[...]).astype(low)
+        wo_part[g, :, :, 0:features] = grads.reshape(split, piece_rows, features)
+        smalls = d_small[columns, :].astype(low)
+        wo_part[g, :, :, features : features + 128] = smalls.reshape(split, piece_rows, 128)
+        return carry
+
+    lax.fori_loop(0, group_count, wo_step, 0)
+    if sums_here:
+        one_start(2)
+    line = LineSum(part, pair_buf, comb, far_buf, pair_send, pair_recv, far_send, far_recv)
+
+    def attend_step(m, carry):
+        for hop in range(cut_count - 1, 0, -1):
+            swap_copy(m, hop).wait()
+        swap_keep(m).wait()
+        attend_back_one(heads, m, qkv_ref, first_ref, lse_ref, back_all, d_qkv, key_acc, value_acc)
+        for c in range(cut_count):
+            part[m, c] = tail_dot(d_qkv[m, c * rows : (c + 1) * rows, :], w_qkv_ref[...]).astype(low)
+        line.start(m)
+        line.forward(m)
+        return carry
+
+    lax.fori_loop(0, micro_count, attend_step, 0)
+
+    def qkv_step(g, carry):
+        columns = pl.ds(pl.multiple_of(g * group_rows, group_rows), group_rows)
+        grads = jnp.zeros((group_rows, 3 * width), f32)
+        for m in range(micro_count):
+            grads = grads + lead_dot(h_all_ref[m, :, columns], d_qkv[m])
+        qkv_part[g] = grads.astype(low).reshape(split, piece_rows, 3 * width)
+        return carry
+
+    lax.fori_loop(0, group_count, qkv_step, 0)
+    if sums_here:
+        one_start(3)
+        in_mid[...] = one_finish(0).astype(low)
+        two_start(0)
+        wo_mid[...] = one_finish(2).astype(low)
+        two_start(2)
+        out_out_ref[...] = one_finish(1)
+
+    def norm_one_step(m, carry):
+        total = line.finish(m)
+        normed, scale = norm_parts(x_ref[m].astype(f32))
+        tokens_ref[m] = d_x_two[m] + norm_back(normed, scale, gain_one_ref[...], total)
+        return carry
+
+    if not sums_here:
+        lax.fori_loop(0, micro_count, norm_one_step, 0)
+        wo_ref[...] = wo_part[...]
+        qkv_out_ref[...] = qkv_part[...]
+        return
+    norm_one_step(0, 0)
+    qkv_mid[...] = one_finish(3).astype(low)
+    two_start(3)
+    two_finish(0)
+    share_piece = in_end.shape[2] // group_count
+    for c in range(cut_count):
+        for g in range(group_count):
+            spot = (g * cut_count + c) * share_piece
+            in_out_ref[:, spot : spot + share_piece] = in_end[c, :, g * share_piece : (g + 1) * share_piece].astype(f32)
+    two_finish(2)
+    total = wo_end[0].astype(f32)
+    for c in range(1, cut_count):
+        total = total + wo_end[c].astype(f32)
+    wo_ref[...] = total[:, :features]
+    small_out_ref[...] = total[:, features:]
+    for m in range(1, micro_count):
+        norm_one_step(m, 0)
+    two_finish(3)
+    norm = jnp.zeros((piece_rows, 1), f32)
+    for c in range(cut_count):
+        for k in range(3):
+            grad = qkv_end[c, :, k * width : (k + 1) * width].astype(f32)
+            qkv_out_ref[k, :, c * width : (c + 1) * width] = grad
+            weights = w_rows_ref[k, :, c * width : (c + 1) * width].astype(f32)
+            norm = norm + jnp.sum(grad * weights, axis=-1, keepdims=True)
+    norm_ref[...] = jnp.broadcast_to(norm, norm_ref.shape)
+
+
+def back(
+    dh, dots, chosen, h_two, x_two, gy, attended, w_output, qkv, first, lse, w_qkv, h_all, x, gain_one, gain_two, small,
+    own_in, own_out, w_rows, heads, expert_count, sums_here, call_id,
+):
+    micro_count, rows, features = x.shape
+    length = qkv.shape[1]
+    cut_count = length // rows
+    width = features // cut_count
+    group_count = own_out.shape[0]
+    piece_rows = features // (group_count * cut_count)
+    share, piece = own_in.shape[3], own_out.shape[1]
+    low, f32 = jnp.bfloat16, jnp.float32
+    levels = cut_count // 2
+    wide = features + 128
+    shape = jax.ShapeDtypeStruct
+    parts = (group_count, cut_count, piece_rows) if sums_here else (features // 256, 1, 256)
+    if sums_here:
+        outs = (
+            shape((micro_count, rows, features), f32), shape((piece_rows, features), f32), shape((piece_rows, 128), f32),
+            shape((3, piece_rows, features), f32), shape((piece_rows, share * cut_count), f32), shape((piece, features), f32),
+            shape((piece_rows, 128), f32),
+        )
+    else:
+        outs = (
+            shape((micro_count, rows, features), f32), shape((*parts, wide), low),
+            shape((8, 128), f32), shape((*parts, 3 * width), low), shape((8, 128), f32),
+            shape((8, 128), f32), shape((8, 128), f32),
+        )
+    peers = max(group_count - 1, 1) if sums_here else 1
+    block = lambda *dims: pltpu.VMEM(dims, low)
+    mids = lambda w: block(cut_count, piece_rows, w) if sums_here else block(16, 128)
+    ins = lambda w: block(peers, cut_count, piece_rows, w) if sums_here else block(16, 128)
+    dma = pltpu.SemaphoreType.DMA
+    vmem = pl.BlockSpec(memory_space=pltpu.VMEM)
+    operands = (
+        dh, dots, chosen, h_two, x_two, gy, attended, w_output, qkv, first, lse, w_qkv, h_all, x, gain_one, gain_two, small,
+        own_in, own_out, w_rows,
+    )
     return pl.pallas_call(
-        partial(attend_back_kernel, heads),
-        grid=(micro_count,),
-        out_shape=jax.ShapeDtypeStruct((micro_count, length, 3 * width), jnp.bfloat16),
-        in_specs=[block(3 * width), block(1), block(width), block(width)],
-        out_specs=block(3 * width),
-        scratch_shapes=[pltpu.VMEM((length, width), jnp.float32), pltpu.VMEM((length, width), jnp.float32)],
-        compiler_params=pltpu.CompilerParams(vmem_limit_bytes=48 * 2**20),
-    )(qkv, first, lse, back)
-
-
-def norm_parts(values):
-    center = values - jnp.mean(values, axis=-1, keepdims=True)
-    spread = jnp.mean(center * center, axis=-1, keepdims=True)
-    scale = lax.rsqrt(spread + norm_eps)
-    return center * scale, scale
-
-
-def norm_back(normed, scale, gain, grad):
-    inner = grad * gain
-    return scale * (
-        inner
-        - jnp.mean(inner, axis=-1, keepdims=True)
-        - normed * jnp.mean(inner * normed, axis=-1, keepdims=True)
-    )
-
-
-def gelu_pair(values):
-    phi = 0.5 * (1.0 + lax.erf(values * (0.5**0.5)))
-    bell = jnp.exp(-0.5 * values * values) * ((2.0 * jnp.pi) ** -0.5)
-    return values * phi, phi + values * bell
-
-
-def softmax_back(probs, grad):
-    return probs * (grad - jnp.sum(probs * grad, axis=-1, keepdims=True))
+        partial(back_kernel, heads, expert_count, sums_here),
+        out_shape=outs,
+        in_specs=[vmem] * len(operands),
+        out_specs=[vmem] * len(outs),
+        scratch_shapes=[
+            pltpu.VMEM((micro_count, rows, features), f32),
+            block(micro_count * rows, features),
+            block(micro_count, rows, features),
+            block(micro_count, length, width),
+            block(micro_count, length, 3 * width),
+            pltpu.VMEM((length, width), f32),
+            pltpu.VMEM((length, width), f32),
+            pltpu.VMEM((features, 128), f32),
+            block(micro_count, cut_count, rows, features),
+            block(micro_count, levels, rows, features),
+            block(micro_count, levels, rows, features),
+            block(micro_count, levels, rows, features),
+            block(*parts, wide),
+            block(*parts, 3 * width),
+            ins(wide), ins(3 * width), ins(share),
+            block(peers, piece, features) if sums_here else block(16, 128),
+            mids(wide), mids(3 * width), mids(share), mids(wide), mids(3 * width), mids(share),
+            dma((micro_count, levels)), dma((micro_count, levels)), dma((micro_count, levels)), dma((micro_count, levels)),
+            dma((micro_count, cut_count)), dma((micro_count, cut_count)), dma((micro_count,)),
+            dma((4, peers)), dma((4, peers)), dma((4, cut_count)), dma((4, cut_count)), dma((4,)),
+        ],
+        compiler_params=pltpu.CompilerParams(
+            collective_id=call_id, has_side_effects=True, vmem_limit_bytes=60 * 2**20
+        ),
+    )(*operands)
 
 
 def local(
@@ -410,7 +843,6 @@
     share = hidden_count // cut_count
     piece = share // group_count
     capacity = max(2, row_count * 5 // (4 * expert_count))
-    slots = expert_count * capacity
     gain_one = norm1_gain.astype(jnp.float32)
     gain_two = norm2_gain.astype(jnp.float32)
     f32, low = jnp.float32, jnp.bfloat16
@@ -433,135 +865,72 @@
     ).reshape(share, features)
 
     x_rows = tokens[0].astype(f32)
-    norm_one, scale_one = norm_parts(x_rows)
+    norm_one, _ = norm_parts(x_rows)
     h_one = (norm_one * gain_one).astype(low)
     h_all = cut_gather(h_one, cut_count, 1).reshape(micro_count, length, features)
     qkv = jnp.einsum("mtf,fk->mtk", h_all, w_qkv, preferred_element_type=f32).astype(low)
     att_part, lse = attend(qkv, first, heads)
     attended = cut_swap(att_part, cut_count, True, 2).reshape(-1, features)
     x_two = x_rows.reshape(-1, features) + plain_dot(attended, w_output)
-    norm_two, scale_two = norm_parts(x_two)
+    norm_two, _ = norm_parts(x_two)
     h_two = (norm_two * gain_two).astype(low)
     h2_all = cut_gather(h_two.reshape(micro_count, row_count, features), cut_count, 3).reshape(-1, features)
     g_all = grad_all.reshape(-1, features)
-    gy_all = g_all.astype(f32)
     tokens_all = micro_count * length
 
-    code_all = codes.reshape(tokens_all)
-    chosen = jnp.where(code_all >= 0, code_all // capacity, -1)
-    hot = (chosen[:, None] == jnp.arange(expert_count, dtype=jnp.int32)[None, :]).astype(f32)
-    routed = softmax_rows(plain_dot(h2_all, router))
-    gate = jnp.sum(hot * routed, axis=-1, keepdims=True)
-    mixing = softmax_rows(plain_dot(h2_all, mixer))
-    mix_gate = mixing[:, 1:2] * gate
-
-    pre = plain_dot(h2_all, own_in)
-    act, slope = gelu_pair(pre)
-    hidden = act.astype(low)
-    dense_part = plain_dot(hidden, own_out)
-    g_dense = (mixing[:, 0:1] * gy_all).astype(low)
-    d_pre = (tail_dot(g_dense, own_out) * slope).astype(low)
-    d_own_in = lead_dot(h2_all, d_pre)
-    d_own_out = lead_dot(hidden, g_dense)
-
-    blocks = tokens_all // row_count
-    table = (code_all.reshape(blocks, row_count, 1) == jnp.arange(slots, dtype=jnp.int32)).astype(low)
-    to_slots = lambda rows: (
-        jnp.einsum("btc,btd->bcd", table, rows.reshape(blocks, row_count, features), preferred_element_type=f32)
-        .astype(low)
-        .reshape(blocks, expert_count, capacity, features)
-        .transpose(1, 0, 2, 3)
-        .reshape(expert_count, blocks * capacity, features)
-    )
-    to_rows = lambda rows: jnp.einsum(
-        "btc,bcd->btd",
-        table,
-        rows.reshape(expert_count, blocks, capacity, features).transpose(1, 0, 2, 3).reshape(blocks, slots, features),
-        preferred_element_type=f32,
-    ).reshape(tokens_all, features)
-    batched = lambda spec, a, b: jnp.einsum(spec, a, b, preferred_element_type=f32)
-    sent = to_slots(h2_all)
-    g_sent = to_slots((mix_gate * gy_all).astype(low))
-    e_pre = batched("etf,efk->etk", sent, weights_in)
-    e_act, e_slope = gelu_pair(e_pre)
-    inner = e_act.astype(low)
-    returned = batched("etk,ekf->etf", inner, weights_out).astype(low)
-    d_e_pre = (batched("etf,ekf->etk", g_sent, weights_out) * e_slope).astype(low)
-    d_sent = batched("etk,efk->etf", d_e_pre, weights_in).astype(low)
-    d_weights_in = batched("etf,etk->efk", sent, d_e_pre).astype(low)
-    d_weights_out = batched("etk,etf->ekf", inner, g_sent).astype(low)
-    fe_part = to_rows(returned)
-
-    dots = jnp.stack([jnp.sum(gy_all * dense_part, axis=-1), jnp.sum(gy_all * fe_part, axis=-1)], axis=-1)
-    dots = lax.psum_scatter(
-        dots.reshape(micro_count, length, 2), "cuts", scatter_dimension=1, tiled=True
-    ).reshape(-1, 2)
-    d_h2_part = (tail_dot(d_pre, own_in) + to_rows(d_sent)).astype(low)
-    d_h2 = cut_scatter(d_h2_part.reshape(micro_count, cut_count, row_count, features), 4).reshape(-1, features)
-    out_part = (mixing[:, 0:1] * dense_part + mix_gate * fe_part).astype(low)
+    tile = 2 * row_count
+    slots = tile_slots(capacity, row_count, tile)
+    kept = codes >= 0
+    chosen = jnp.where(kept, codes // capacity, -1)
+    parity = (jnp.arange(length, dtype=jnp.int32) // row_count) % 2
+    spot = jnp.where(kept, chosen * slots + parity * capacity + codes % capacity, -1).reshape(tokens_all, 1)
+    small = jnp.concatenate([router, mixer, jnp.zeros((features, 126 - expert_count), low)], axis=1)
+    out_part, d_h2_part, dots, d_own_in, d_own_out, d_weights_in, d_weights_out = feed(
+        h2_all, g_all, chosen.reshape(tokens_all, 1), spot, small, own_in, own_out, weights_in, weights_out, tile, slots
+    )
+    dots = dots.reshape(micro_count, cut_count, 8, row_count).transpose(1, 0, 2, 3)
+    d_h2, dots = cut_scatter(d_h2_part.reshape(micro_count, cut_count, row_count, features), dots, 4)
     out_sum = lax.psum_scatter(
         out_part.reshape(micro_count, length, features), "cuts", scatter_dimension=1, tiled=True
     )
     output = (x_two.reshape(out_sum.shape) + out_sum.astype(f32)).astype(low)
 
-    mine = lambda rows: lax.dynamic_slice_in_dim(
-        rows.reshape(micro_count, length, -1), cut * row_count, row_count, 1
-    ).reshape(micro_count * row_count, -1)
-    gy = cotangent[0].reshape(-1, features).astype(f32)
-    own_gate, own_mixing, own_hot, own_routed = mine(gate), mine(mixing), mine(hot), mine(routed)
-    d_mixing = jnp.concatenate([dots[:, 0:1], own_gate * dots[:, 1:2]], axis=1)
-    d_mixer_logits = softmax_back(own_mixing, d_mixing)
-    d_router_logits = softmax_back(own_routed, own_hot * (own_mixing[:, 1:2] * dots[:, 1:2]))
-    small = jnp.concatenate([router, mixer], axis=1).astype(f32)
-    d_logits = jnp.concatenate([d_router_logits, d_mixer_logits], axis=1)
-    d_h2 = d_h2 + lax.dot_general(d_logits, small, (((1,), (1,)), ((), ())), preferred_element_type=f32)
-    d_small = lead_dot(h_two.astype(f32), d_logits)
-    d_gain_two = jnp.sum(d_h2 * norm_two, axis=0)
-    d_x_two = gy + norm_back(norm_two, scale_two, gain_two, d_h2)
-    g_att = d_x_two.astype(low)
-    d_output = lead_dot(attended, g_att)
-    d_att = tail_dot(g_att, w_output).astype(low).reshape(micro_count, row_count, features)
-    d_att_part = cut_swap(d_att, cut_count, False, 5)
-    d_qkv = attend_back(qkv, first, lse, d_att_part, heads)
-    d_w_qkv = lead_dot(h_all.reshape(tokens_all, features), d_qkv.reshape(tokens_all, -1))
-    d_h1_part = tail_dot(d_qkv.reshape(tokens_all, -1), w_qkv).astype(low)
-    d_h1 = cut_scatter(d_h1_part.reshape(micro_count, cut_count, row_count, features), 6)
-    grad_tokens = d_x_two.reshape(d_h1.shape) + norm_back(norm_one, scale_one, gain_one, d_h1)
-
     rows = features // (group_count * cut_count)
-    grad_expert_in = lax.psum_scatter(d_weights_in, "expert", scatter_dimension=0).astype(f32)
-    grad_expert_out = lax.psum_scatter(d_weights_out, "expert", scatter_dimension=0).astype(f32)
-    grad_dense_out = lax.psum_scatter(d_own_out.astype(low), "expert", scatter_dimension=0, tiled=True).astype(f32)
-
-    def to_owner(part):
-        summed = lax.psum_scatter(part.astype(low), "expert", scatter_dimension=0, tiled=True)
-        return lax.all_to_all(summed.reshape(cut_count, rows, -1), "cuts", split_axis=0, concat_axis=0)
-
-    grad_dense_in = (
-        to_owner(d_own_in).astype(f32)
-        .reshape(cut_count, rows, group_count, piece)
-        .transpose(1, 2, 0, 3)
-        .reshape(rows, hidden_count)
-    )
-    grad_qkv = to_owner(d_w_qkv).astype(f32).reshape(cut_count, rows, 3, head_width).transpose(2, 1, 0, 3)
-    grad_qkv = grad_qkv.reshape(3, rows, features)
-    wide = jnp.concatenate([d_output, d_small, d_gain_two[:, None]], axis=1).astype(low)
-    wide = wide.reshape(group_count, cut_count, rows, -1).transpose(1, 0, 2, 3)
-    wide = lax.psum_scatter(wide, "cuts", scatter_dimension=0)
-    wide = lax.psum_scatter(wide, "expert", scatter_dimension=0).astype(f32)
-    grad_output = wide[:, :features]
-    grad_router = wide[:, features : features + expert_count]
-    grad_mixer = wide[:, features + expert_count : -1]
-    grad_norm2 = wide[:, -1]
-
+    sums_here = rows % 16 == 0
+    own_chosen = jnp.where(code >= 0, code // capacity, -1)[..., None]
+    by_micro = lambda a: a.reshape(micro_count, row_count, features)
     place = (lax.axis_index("expert") * cut_count + cut) * rows
-    own_rows = lambda w: lax.dynamic_slice_in_dim(w, place, rows, 0).astype(f32)
-    grad_norm1 = sum(
-        jnp.sum(own_rows(w) * grad_qkv[k], axis=-1) for k, w in enumerate((w_query, w_key, w_value))
-    ) / own_rows(gain_one)
+    own_rows = lambda w: lax.dynamic_slice_in_dim(w, place, rows, 0)
+    w_rows = jnp.stack([own_rows(w) for w in (w_query, w_key, w_value)])
+    grad_tokens, grad_output, grad_small, grad_qkv, grad_dense_in, grad_dense_out, norm_sum = back(
+        d_h2, dots, own_chosen, by_micro(h_two), by_micro(x_two), cotangent[0], attended, w_output, qkv, first, lse, w_qkv,
+        h_all, tokens[0], gain_one[None], gain_two[None], small,
+        d_own_in.reshape(group_count, cut_count, rows, share), d_own_out.reshape(group_count, piece, features), w_rows,
+        heads, expert_count, sums_here, 5,
+    )
+    sum_groups = lambda part: lax.psum_scatter(
+        part.reshape(-1, part.shape[-1]), "expert", scatter_dimension=0, tiled=True
+    )
+    grad_expert_in = sum_groups(d_weights_in).astype(f32)
+    grad_expert_out = sum_groups(d_weights_out).astype(f32)
+    if not sums_here:
+        swap = lambda part: lax.all_to_all(
+            part.reshape(cut_count, rows, -1), "cuts", split_axis=0, concat_axis=0
+        ).astype(f32)
+        wide = jnp.sum(swap(sum_groups(grad_output)), axis=0)
+        grad_output, grad_small = wide[:, :features], wide[:, features:]
+        grad_qkv = swap(sum_groups(grad_qkv)).reshape(cut_count, rows, 3, head_width).transpose(2, 1, 0, 3)
+        grad_qkv = grad_qkv.reshape(3, rows, features)
+        grad_dense_in = swap(sum_groups(d_own_in)).reshape(cut_count, rows, group_count, piece).transpose(1, 2, 0, 3)
+        grad_dense_in = grad_dense_in.reshape(rows, hidden_count)
+        grad_dense_out = sum_groups(d_own_out).astype(f32)
+        norm_sum = jnp.sum(grad_qkv * w_rows.astype(f32), axis=(0, 2))[:, None]
+
+    grad_norm1 = norm_sum[:, 0] / own_rows(gain_one)
     return (
-        output[None], grad_tokens[None], grad_norm1, grad_qkv[0], grad_qkv[1], grad_qkv[2], grad_output, grad_norm2,
-        grad_dense_in, grad_dense_out, grad_router, grad_mixer, grad_expert_in[None], grad_expert_out[None],
+        output[None], grad_tokens[None], grad_norm1, grad_qkv[0], grad_qkv[1], grad_qkv[2], grad_output,
+        grad_small[:, expert_count + 2], grad_dense_in, grad_dense_out, grad_small[:, :expert_count],
+        grad_small[:, expert_count : expert_count + 2], grad_expert_in[None], grad_expert_out[None],
     )
 
 

time: 731 us -> 454 us (0.62)
  waiting for transfers between devices: 202 us -> 36.7 us
  matrix products: 124 us -> 5.32 us
  Pallas kernels: 265 us -> 314 us
  local copies, waits for them, and re-layouts: 65.1 us -> 49.5 us
  other arithmetic: 29.1 us -> 14.8 us
    unnamed x17 -> x6, waiting for transfers between devices: 141 us -> 3.11 us
    dot_general x20 -> x0, matrix products: 101 us -> none  [the longest x6 45.1 us: local(): jnp.einsum(spec, a, b, preferred_element_type=f32)]
    pallas_call x3, Pallas kernels: 112 us -> 210 us  [the longest x1 101 us: back(): pl.pallas_call(partial(back_kernel, heads, expert_count, sums_here), out_...]
    pallas_call x2, Pallas kernels: 108 us -> 79.2 us  [cut_gather(): pl.pallas_call(partial(gather_kernel, chain), out_shape=jax.ShapeDtypeStr...]
    pallas_call x2 -> x1, Pallas kernels: 36.1 us -> 15.5 us  [cut_swap(): pl.pallas_call(partial(swap_kernel, to_rows), out_shape=jax.ShapeDtypeStr...]
    dot_general x5 -> x1, matrix products: 20.7 us -> 0.79 us  [plain_dot(): return jnp.dot(left, right, preferred_element_type=jnp.float32)]
    reduce_scatter x1, waiting for transfers between devices: 49.5 us -> 31.8 us  [local(): lax.psum_scatter(out_part.reshape(micro_count, length, features), 'cuts',...]
    convert_element_type x5 -> x0, other arithmetic: 9.05 us -> none  [the longest x1 2.83 us: local(): lax.psum_scatter(d_weights_in, 'expert', scatter_dimension=0).astype(f32)]
  transfers between devices with their start and end apart: 14 -> 6, of which waited for: 6 -> 2; matrix products, arithmetic and copies ran while one was open for 22% -> 12% of each run, Pallas kernels for 37% -> 57%
where the time goes in v2:
time: 454 us; the launch traced here: 446 us
  Pallas kernels  314 us (69%)
  local copies, waits for them, and re-layouts  49.5 us (11%)
  waiting for transfers between devices  36.7 us (8%)
  between operations  14.9 us (3%)
  other arithmetic  14.8 us (3%)
  blocking collectives  10.9 us (2%)
  matrix products  5.32 us (1%)
    pallas_call x1, Pallas kernels, back(): pl.pallas_call(partial(back_kernel, heads, expert_count, sums_here), out_...  101 us
    pallas_call x2, Pallas kernels, cut_gather(): pl.pallas_call(partial(gather_kernel, chain), out_shape=jax.ShapeDtypeStr...  79.2 us
    pallas_call x1, Pallas kernels, feed(): pl.pallas_call(partial(feed_kernel, tile, slots), grid=(expert_count + 2,...  58.1 us
    pallas_call x1, Pallas kernels, cut_scatter(): pl.pallas_call(scatter_kernel, out_shape=(jax.ShapeDtypeStruct((micro_cou...  51.3 us
    reduce_scatter x1, waiting for transfers between devices, local(): lax.psum_scatter(out_part.reshape(micro_count, length, features), 'cuts',...  31.8 us
    unnamed x84, local copies, waits for them, and re-layouts  28.9 us
    pallas_call x1, Pallas kernels, cut_swap(): pl.pallas_call(partial(swap_kernel, to_rows), out_shape=jax.ShapeDtypeStr...  15.5 us
    all_gather x1, blocking collectives, local(): codes = lax.all_gather(code, 'cuts', axis=1, tiled=True)  10.9 us
  transfers between devices with their start and end apart: 6, of which 2 were waited for; matrix products, arithmetic and copies ran while one was open for 12% of the time, Pallas kernels for 57%

profile of v2, /device:TPU:0, one launch (start us, length us, event | category | flops | bytes accessed | tf_op | source)
XLA Modules:
  0.0 446.1 jit_solution(6485183116466535359)
XLA Ops:
  10.3 41.5 %shard_map.281 = bf16[2,8,128,1024]{3,2,1,0:T(8,128)(2,1)S(1)} custom-call(bf16[2,128,1024]{2,1,0:T(8,128)(2,1)S(1)} %fusion.4.x_ref), custom_call_target="tpu_custom_call" | custom-call | tf_op jit(solution)/shard_map/pallas_call | solution.py:131
  51.8 2.0 copy-done.1
  55.4 1.4 constant_dynamic-slice_fusion.1
  57.6 4.5 %convolution_convert_fusion.qkv_ref = bf16[2,1024,384]{2,1,0:T(8,128)(2,1)S(1)} fusion(bf16[2,1024,1024]{2,1,0:T(8,128)(2,1)} %bitcast.107, bf16[1024,128]{1,0:T(8,128)(2,1)S(1)} %get-tuple-element.159, bf16[1024,128]{1,0:T(8,128)(2,1)S(1)} %get-tuple-element.160, bf16[1024,128]{1,0:T(8,128)(2,1)S(1)} %constant_dynamic-slice_fusion.3), kind=kOutput, calls=%fused_computation.2 | convolution fusion | flops 1613758464 | bytes 6553600 | tf_op jit(solution)/shard_map/mtf,fk->mtk/dot_general | solution.py:871
  62.2 8.8 %shard_map.282 = (bf16[2,1024,128]{2,1,0:T(8,128)(2,1)S(1)}, f32[2,1024,128]{2,1,0:T(8,128)S(1)}) custom-call(bf16[2,1024,384]{2,1,0:T(8,128)(2,1)S(1)} %convolution_convert_fusion.qkv_ref, s32[2,1024,1]{2,1,0:T(8,128)S(1)} %copy.113.first_ref), custom_call_target="tpu_custom_call" | custom-call | tf_op jit(solution)/shard_map/pallas_call | solution.py:295
  71.0 15.5 %shard_map.283 = bf16[2,128,1024]{2,1,0:T(8,128)(2,1)S(1)} custom-call(bf16[2,1024,128]{2,1,0:T(8,128)(2,1)S(1)} %get-tuple-element.32.x_ref), custom_call_target="tpu_custom_call" | custom-call | tf_op jit(solution)/shard_map/pallas_call | solution.py:240
  88.4 37.7 %shard_map.284 = bf16[2,8,128,1024]{3,2,1,0:T(8,128)(2,1)S(1)} custom-call(bf16[2,128,1024]{2,1,0:T(8,128)(2,1)S(1)} %bitcast.112), custom_call_target="tpu_custom_call" | custom-call | tf_op jit(solution)/shard_map/pallas_call | solution.py:131
  126.2 2.1 copy-done.2
  128.2 10.0 %copy.134 = bf16[128,8,32,128]{3,2,1,0:T(8,128)(2,1)} copy(bf16[128,8,32,128]{3,1,2,0:T(8,128)(2,1)} %bitcast.121) | data formatting | bytes 16777216
  138.2 10.3 %dynamic-slice_reduce_fusion = bf16[1024,4,128]{2,1,0:T(4,128)(2,1)S(1)} fusion(bf16[1024,4,8,128]{3,2,1,0:T(8,128)(2,1)} %bitcast.118, s32[]{:T(128)S(6)} %select_n.101), kind=kLoop, calls=%fused_computation.1 | loop fusion | bytes 2097156 | tf_op jit(solution)/shard_map/jit(dynamic_index_in_dim)/dynamic_slice | solution.py:860
  149.7 10.9 %all-gather.1 = s32[1,2,1024]{2,1,0:T(2,128)S(1)} all-gather(s32[1,2,128]{2,1,0:T(2,128)S(1)} %get-tuple-element.149), channel_id=3, replica_groups=mesh['expert'=4,'cuts'=8] {'cuts'}, dimensions={2}, use_global_device_ids=true | all-gather | bytes 9216 | tf_op jit(solution)/shard_map/all_gather | solution.py:851
  163.9 2.2 constant_dynamic-slice_fusion
  167.1 1.7 all-gather.10.cloned.1.call-done
  168.8 58.1 %shard_map.285 = (bf16[2048,1024]{1,0:T(8,128)(2,1)}, bf16[2048,1024]{1,0:T(8,128)(2,1)}, f32[16,8,128]{2,1,0:T(8,128)}, bf16[1024,512]{1,0:T(8,128)(2,1)}, bf16...) custom-call(bf16[2048,1024]{1,0:T(8,128)(2,1)} %bitcast.109, ...), custom_call_target="tpu_custom_call" | custom-call | tf_op jit(solution)/shard_map/pallas_call | solution.py:446
  232.0 2.4 copy-done.7
  234.4 51.3 %shard_map.286 = (f32[2,128,1024]{2,1,0:T(8,128)S(1)}, f32[2,8,128]{2,1,0:T(8,128)S(1)}) custom-call(bf16[2,8,128,1024]{3,2,1,0:T(8,128)(2,1)S(1)} %bitcast.114, f32[8,2,8,128]{3,2,1,0:T(8,128)S(1)} %bitcast.115), custom_call_target="tpu_custom_call" | custom-call | tf_op jit(solution)/shard_map/pallas_call | solution.py:180
  287.2 100.9 %shard_map.287 = (f32[2,128,1024]{2,1,0:T(8,128)}, f32[32,1024]{1,0:T(8,128)}, f32[32,128]{1,0:T(8,128)}, f32[3,32,1024]{2,1,0:T(8,128)}, f32[32,4096]{1,0:T(8,1...) custom-call(f32[2,128,1024]{2,1,0:T(8,128)} %copy-done.9, f32[2,8,128]{2,1,0:T(8,128)} %copy-done.10, ...), custom_call_target="tpu_custom_call" | custom-call | tf_op jit(solution)/shard_map/pallas_call | solution.py:797
  389.5 1.4 copy.126
  390.9 1.4 slice_reduce_fusion
  394.4 1.8 slice_bitcast_fusion
  396.2 2.8 bitcast_convert_fusion
  399.0 2.9 bitcast_convert_fusion.1
  402.0 31.8 %reduce-scatter.4.cloned.1.call-done = bf16[2,128,1024]{2,1,0:T(8,128)(2,1)} async-done(((bf16[2,1024,1024]{2,1,0:T(8,128)(2,1)}), bf16[2,128,1024]{2,1,0:T(8,128)(2,1)}) %reduce-scatter.4.cloned.1.call-update) | async-done | bytes 524304 | tf_op jit(solution)/shard_map/reduce_scatter | solution.py:893
  433.8 2.1 fusion.6
  (129 shorter events, 25.7 us)
Async XLA Ops:
  7.2 48.2 %copy-start = (bf16[1024,1024]{1,0:T(8,128)(2,1)S(1)}, bf16[1024,1024]{1,0:T(8,128)(2,1)}, u32[]{:S(2)}) copy-start(bf16[1024,1024]{1,0:T(8,128)(2,1)} %param.25) | copy-start | bytes 6291460
  7.2 159.8 %all-gather.6.cloned.1.call-start = ((), (), s32[]{:S(2)}) async-start(), calls=%async_computation.3 | async-start | bytes 5242880 | tf_op jit(solution)/shard_map/all_gather | solution.py:855
  8.0 159.1 %all-gather.8.cloned.1.call-start = ((), (), s32[]{:S(2)}) async-start(), calls=%async_computation.4 | async-start | bytes 5242880 | tf_op jit(solution)/shard_map/all_gather | solution.py:856
  8.7 160.1 %all-gather.10.cloned.1.call-start = ((), (), s32[]{:S(2)}) async-start(), calls=%async_computation.8 | async-start | bytes 4718592 | tf_op jit(solution)/shard_map/all_gather | solution.py:854
  9.4 386.8 %reduce-scatter.8.cloned.1.call-start = ((), (), s32[]{:S(2)}) async-start(), calls=%async_computation.7 | async-start | bytes 5242880 | tf_op jit(solution)/shard_map/reduce_scatter | solution.py:911
  9.5 42.3 %copy-start.25 = (f32[1024]{0:T(1024)}, f32[1024]{0:T(1024)S(1)}, u32[]{:S(2)}) copy-start(f32[1024]{0:T(1024)S(1)} %convert_element_type.38) | copy-start | bytes 12292
  10.3 43.5 %copy-start.27 = (s32[1,2,1024]{2,1,0:T(2,128)S(1)}, s32[1,2,1024]{2,1,0:T(2,128)}, u32[]{:S(2)}) copy-start(s32[1,2,1024]{2,1,0:T(2,128)} %param.20) | copy-start | bytes 24580
  55.3 6.8 %copy-start.3 = (s32[2,1024,1]{2,1,0:T(8,128)}, s32[2,1024,1]{2,1,0:T(8,128)S(1)}, u32[]{:S(2)}) copy-start(s32[2,1024,1]{2,1,0:T(8,128)S(1)} %copy.113.first_ref) | copy-start | bytes 24580
  62.1 8.9 %copy-start.4 = (bf16[2,1024,384]{2,1,0:T(8,128)(2,1)}, bf16[2,1024,384]{2,1,0:T(8,128)(2,1)S(1)}, u32[]{:S(2)}) copy-start(bf16[2,1024,384]{2,1,0:T(8,128)(2,1)S(1)} %convolution_convert_fusion.qkv_ref) | copy-start | bytes 4718596
  62.1 24.4 %copy-start.31 = (bf16[1024]{0:T(1024)(128)(2,1)S(1)}, bf16[1024]{0:T(1024)(128)(2,1)}, u32[]{:S(2)}) copy-start(bf16[1024]{0:T(1024)(128)(2,1)} %param.29) | copy-start | bytes 6148
  62.1 24.5 %copy-start.14 = (bf16[1,2,128,1024]{3,2,1,0:T(8,128)(2,1)S(1)}, bf16[1,2,128,1024]{3,2,1,0:T(8,128)(2,1)}, u32[]{:S(2)}) copy-start(bf16[1,2,128,1024]{3,2,1,0:T(8,128)(2,1)} %param.18) | copy-start | bytes 1572868
  62.2 24.5 %copy-start.15 = (bf16[1024,1024]{1,0:T(8,128)(2,1)S(1)}, bf16[1024,1024]{1,0:T(8,128)(2,1)}, u32[]{:S(2)}) copy-start(bf16[1024,1024]{1,0:T(8,128)(2,1)} %w_out_ref.1) | copy-start | bytes 6291460
  71.0 16.4 %copy-start.8 = (f32[2,1024,128]{2,1,0:T(8,128)}, f32[2,1024,128]{2,1,0:T(8,128)S(1)}, u32[]{:S(2)}) copy-start(f32[2,1024,128]{2,1,0:T(8,128)S(1)} %get-tuple-element.38.lse_ref) | copy-start | bytes 3145732
  88.4 37.7 %copy-start.6 = (bf16[256,1024]{1,0:T(8,128)(2,1)}, bf16[256,1024]{1,0:T(8,128)(2,1)S(1)}, u32[]{:S(2)}) copy-start(bf16[256,1024]{1,0:T(8,128)(2,1)S(1)} %multiply_convert_fusion) | copy-start | bytes 1572868
  138.2 11.5 %copy-start.32 = (s32[1,2,128]{2,1,0:T(2,128)S(1)}, s32[1,2,128]{2,1,0:T(2,128)}, u32[]{:S(2)}) copy-start(s32[1,2,128]{2,1,0:T(2,128)} %param.22) | copy-start | bytes 3076
  138.2 11.5 %copy-start.33 = (s32[1,2,128]{2,1,0:T(2,128)S(1)}, s32[1,2,128]{2,1,0:T(2,128)}, u32[]{:S(2)}) copy-start(s32[1,2,128]{2,1,0:T(2,128)} %param.21) | copy-start | bytes 3076
  138.2 11.5 %copy-start.34 = (s32[1,2,128]{2,1,0:T(2,128)S(1)}, s32[1,2,128]{2,1,0:T(2,128)}, u32[]{:S(2)}) copy-start(s32[1,2,128]{2,1,0:T(2,128)} %param.23) | copy-start | bytes 3076
  148.5 14.9 %copy-start.28 = (bf16[1024,4]{0,1:T(4,128)(2,1)S(1)}, bf16[1024,4]{0,1:T(4,128)(2,1)}, u32[]{:S(2)}) copy-start(bf16[1024,4]{0,1:T(4,128)(2,1)} %param.32) | copy-start | bytes 24580
  148.5 15.1 %copy-start.29 = (bf16[1024,2]{0,1:T(2,128)(2,1)S(1)}, bf16[1024,2]{0,1:T(2,128)(2,1)}, u32[]{:S(2)}) copy-start(bf16[1024,2]{0,1:T(2,128)(2,1)} %param.33) | copy-start | bytes 12292
  226.9 172.1 %reduce-scatter.6.cloned.1.call-start = ((), (), s32[]{:S(2)}) async-start(), calls=%async_computation.6 | async-start | bytes 5242880 | tf_op jit(solution)/shard_map/reduce_scatter | solution.py:911
  227.5 206.2 %reduce-scatter.4.cloned.1.call-start = ((), (), s32[]{:S(2)}) async-start(), calls=%async_computation.5 | async-start | bytes 4718592 | tf_op jit(solution)/shard_map/reduce_scatter | solution.py:893
  228.1 3.9 copy-start.24
  399.0 34.7 %copy-start.12 = (f32[256,1024]{1,0:T(8,128)S(1)}, f32[256,1024]{1,0:T(8,128)}, u32[]{:S(2)}) copy-start(f32[256,1024]{1,0:T(8,128)} %copy-done.11) | copy-start | bytes 3145732
  402.0 34.9 %copy-start.23 = (f32[32,1024]{1,0:T(8,128)S(1)}, f32[32,1024]{1,0:T(8,128)}, u32[]{:S(2)}) copy-start(f32[32,1024]{1,0:T(8,128)} %get-tuple-element.183) | copy-start | bytes 393220
  (17 other events, 30.8 us)
Sparse Core Ops, SparseCore 0:
  9.9 55.3 all-gather.5
  67.2 52.6 all-gather.7
  121.5 47.2 all-gather.9
  227.0 51.3 reduce-scatter.7
  281.5 99.9 reduce-scatter.5
  383.7 50.0 reduce-scatter.3
